TPU v7x, 128 devices: a whole 4x4x4 slice. The times are simulated.
128 devices in a mesh: grp: 2 (over y_hi), seq: 64 (over x, z, y_lo, core).
Axes of the slice: x: 4, y: 4 (y_hi: 2, y_lo: 2; y = y_hi * 2 + y_lo), z: 4, core: 2. Of those that a mesh axis runs over, the one named last changes fastest.
Arguments:
- queries: bfloat16 [16384, 2048], P(('grp', 'seq')), parts along dimension 0, may hold values from -150 to 150
- keys: bfloat16 [16384, 1024], P(('grp', 'seq')), parts along dimension 0, may hold values from -6 to 6
- values: bfloat16 [16384, 1024], P(('grp', 'seq')), parts along dimension 0, may hold values from -6 to 6
- dout: bfloat16 [16384, 2048], P(('grp', 'seq')), parts along dimension 0, may hold values from -6 to 6
- tail_keys: bfloat16 [2048, 1024], P(('grp', 'seq')), parts along dimension 0, may hold values from -6 to 6
- tail_values: bfloat16 [2048, 1024], P(('grp', 'seq')), parts along dimension 0, may hold values from -6 to 6
- lengths: int32 [4], P('grp'), parts along dimension 0, may hold values from 1 to 6144, 8192 in all
Outputs:
- grad_queries: bfloat16 [16384, 2048], P(('grp', 'seq')), parts along dimension 0
- grad_keys: bfloat16 [16384, 1024], P(('grp', 'seq')), parts along dimension 0
- grad_values: bfloat16 [16384, 1024], P(('grp', 'seq')), parts along dimension 0
- grad_tail_keys: bfloat16 [2048, 1024], P(('grp', 'seq')), parts along dimension 0
- grad_tail_values: bfloat16 [2048, 1024], P(('grp', 'seq')), parts along dimension 0
There are 2 independent parts, one for each index of `grp`. A program takes and returns all parts, laid end to end along the dimension named above; each array names one. Nothing has to cross between parts.
All inputs are finite; a program needn't handle non-finite values.
Results may differ from a plain program's by a relative error of at most 0.039.
Values may be sent and summed in bfloat16 or wider, within the bound.
A program may use at most 128 MiB of HBM per device.

v0:
```python
import jax
import jax.numpy as jnp
from jax import lax
from jax.sharding import PartitionSpec as P

H = 16
KVH = 8
HD = 128
W = 1024


qscale = 168.0 ** (-0.5)
neg_big = -1e30


def passed_along(value, axis, steps):
    count = lax.axis_size(axis)
    leading, last = (max(0, -steps), min(count, count - steps))
    return lax.ppermute(value, axis, [(source, source + steps) for source in range(leading, last)])


def token_place(glob_rows, lengths):
    finish = jnp.cumsum(lengths)
    starts = finish - lengths
    rollout = jnp.sum((finish[None, :] <= glob_rows[:, None]).astype(jnp.int32), axis=1)
    indices = jnp.arange(lengths.shape[0])
    anchor = jnp.sum(jnp.where(indices[None, :] == rollout[:, None], starts[None, :], 0), axis=1)
    rollout = jnp.where(glob_rows < 0, -1, rollout)
    return (rollout, glob_rows - anchor)


def window_mask(query_glob, query_roll, key_glob, key_roll):
    distance = query_glob[:, None] - key_glob[None, :]
    return (query_roll[:, None] == key_roll[None, :]) & (distance >= 0) & (distance < W)


def tail_mask(query_pos):
    return jnp.arange(W)[None, :] > query_pos[:, None]


def scores(query_heads, key_rows):
    keyset = key_rows.reshape(key_rows.shape[0], KVH, HD)
    return (
        jnp.einsum("rkgd,ckd->kgrc", query_heads, keyset, preferred_element_type=jnp.float32)
        * qscale
    )


def block_stats(query_heads, key_rows, visible):
    live = visible[None, None]
    logits = jnp.where(live, scores(query_heads, key_rows), neg_big)
    blk_max = jnp.max(logits, axis=3)
    blk_sum = jnp.sum(jnp.where(live, jnp.exp(logits - blk_max[..., None]), 0.0), axis=3)
    return (blk_max, blk_sum)


def block_attend(query_heads, dout_heads, key_rows, value_rows, visible, log_total):
    live = visible[None, None]
    attend = jnp.where(live, jnp.exp(scores(query_heads, key_rows) - log_total[..., None]), 0.0)
    valset = value_rows.reshape(value_rows.shape[0], KVH, HD)
    dweight = jnp.einsum("rkgd,ckd->kgrc", dout_heads, valset, preferred_element_type=jnp.float32)
    return (attend, dweight)


def block_delta(query_heads, dout_heads, key_rows, value_rows, visible, log_total):
    attend, dweight = block_attend(
        query_heads, dout_heads, key_rows, value_rows, visible, log_total
    )
    return jnp.sum(attend * dweight, axis=3)


def block_grads(query_heads, dout_heads, key_rows, value_rows, visible, log_total, deltas):
    attend, dweight = block_attend(
        query_heads, dout_heads, key_rows, value_rows, visible, log_total
    )
    dscores = (attend * (dweight - deltas[..., None])).astype(jnp.bfloat16)
    rounded = attend.astype(jnp.bfloat16)
    keyset = key_rows.reshape(key_rows.shape[0], KVH, HD)
    query_grad = (
        jnp.einsum("kgrc,ckd->rkgd", dscores, keyset, preferred_element_type=jnp.float32) * qscale
    )
    key_grad = (
        jnp.einsum("kgrc,rkgd->ckd", dscores, query_heads, preferred_element_type=jnp.float32)
        * qscale
    )
    value_grad = jnp.einsum(
        "kgrc,rkgd->ckd", rounded, dout_heads, preferred_element_type=jnp.float32
    )
    return (query_grad, jnp.stack((key_grad, value_grad)).reshape(2, key_rows.shape[0], KVH * HD))


def on_device(queries, keys, values, dout, tail_keys, tail_values, lengths):
    row_count = queries.shape[0]
    groups = H // KVH
    halo_depth = W // row_count
    own_index = lax.axis_index("seq")
    query_glob = own_index * row_count + jnp.arange(row_count)
    query_roll, query_pos = token_place(query_glob, lengths)
    query_heads = queries.reshape(row_count, KVH, groups, HD)
    dout_heads = dout.reshape(row_count, KVH, groups, HD)
    key_pair = jnp.stack((keys, values))
    arrived = [passed_along(key_pair, "seq", offset) for offset in range(1, halo_depth + 1)]
    gathered_keys, gathered_vals = (
        lax.all_gather(tail_keys, "seq", axis=0, tiled=True),
        lax.all_gather(tail_values, "seq", axis=0, tiled=True),
    )
    blocks = [(keys, values, window_mask(query_glob, query_roll, query_glob, query_roll))]
    for offset in range(1, halo_depth + 1):
        key_glob = query_glob - offset * row_count
        key_roll, key_pos = token_place(key_glob, lengths)
        blocks.append(
            (
                arrived[offset - 1][0],
                arrived[offset - 1][1],
                window_mask(query_glob, query_roll, key_glob, key_roll),
            )
        )
    blocks.append((gathered_keys, gathered_vals, tail_mask(query_pos)))
    head_shape = (KVH, groups, row_count)
    run_max = jnp.full(head_shape, neg_big, jnp.float32)
    run_sum = jnp.zeros(head_shape, jnp.float32)
    for key_rows, value_rows, visible in blocks:
        blk_max, blk_sum = block_stats(query_heads, key_rows, visible)
        new_max = jnp.maximum(run_max, blk_max)
        run_sum = run_sum * jnp.exp(run_max - new_max) + blk_sum * jnp.exp(blk_max - new_max)
        run_max = new_max
    log_total = run_max + jnp.log(run_sum)
    deltas = jnp.zeros(head_shape, jnp.float32)
    for key_rows, value_rows, visible in blocks:
        deltas = deltas + block_delta(
            query_heads, dout_heads, key_rows, value_rows, visible, log_total
        )
    query_zero = jnp.zeros((row_count, KVH, groups, HD), jnp.float32)
    query_grad = query_zero
    grads = []
    for key_rows, value_rows, visible in blocks:
        block_query, block_kv = block_grads(
            query_heads, dout_heads, key_rows, value_rows, visible, log_total, deltas
        )
        query_grad = query_grad + block_query
        grads.append(block_kv)
    partials = grads[1 : halo_depth + 1]
    tail_part = grads[halo_depth + 1]
    returned = sum(
        [
            passed_along(partials[offset - 1].astype(jnp.bfloat16), "seq", -offset).astype(
                jnp.float32
            )
            for offset in range(1, halo_depth + 1)
        ]
    )
    merged = grads[0] + returned
    tail_key_grad, tail_value_grad = (
        lax.psum_scatter(tail_part[0], "seq", scatter_dimension=0, tiled=True),
        lax.psum_scatter(tail_part[1], "seq", scatter_dimension=0, tiled=True),
    )
    return (
        query_grad.reshape(row_count, H * HD).astype(jnp.bfloat16),
        merged[0].astype(jnp.bfloat16),
        merged[1].astype(jnp.bfloat16),
        tail_key_grad.astype(jnp.bfloat16),
        tail_value_grad.astype(jnp.bfloat16),
    )


def solution(mesh):
    placed = (
        P(("grp", "seq"), None),
        P(("grp", "seq"), None),
        P(("grp", "seq"), None),
        P(("grp", "seq"), None),
        P(("grp", "seq"), None),
        P(("grp", "seq"), None),
        P("grp"),
    )
    return jax.shard_map(
        on_device,
        mesh=mesh,
        in_specs=placed,
        out_specs=(
            P(("grp", "seq"), None),
            P(("grp", "seq"), None),
            P(("grp", "seq"), None),
            P(("grp", "seq"), None),
            P(("grp", "seq"), None),
        ),
        check_vma=False,
    )
```

profile of v0, /device:TPU:1, one launch (start us, length us, event | category | flops | bytes accessed | tf_op | source)
XLA Modules:
  0.0 893.1 jit_solution(11392900039659747135)
XLA Ops:
  11.0 6.3 collective-permute-start.7
  17.4 3.8 collective-permute-start.6
  21.2 4.5 collective-permute-start.5
  25.8 4.8 collective-permute-start.4
  41.4 10.4 %collective-permute-done.7 = bf16[2,128,1024]{1,2,0:T(8,128)(2,1)S(1)} collective-permute-done((bf16[2,128,1024]{1,2,0:T(8,128)(2,1)}, bf16[2,128,1024]{1,2,0:T(8,128)(2,1)S(1)}, u32[]{:S(2)}, u32[]{:S(2)}) %collective-permute-start.7) | collective-permute-done | bytes 524320 | tf_op jit(solution)/shard_map/ppermute | solution.py:19
  51.8 5.2 collective-permute-start.2
  58.4 28.7 %collective-permute-done.6 = bf16[2,128,1024]{1,2,0:T(8,128)(2,1)} collective-permute-done((bf16[2,128,1024]{1,2,0:T(8,128)(2,1)}, bf16[2,128,1024]{1,2,0:T(8,128)(2,1)}, u32[]{:S(2)}, u32[]{:S(2)}) %collective-permute-start.6) | collective-permute-done | bytes 524320 | tf_op jit(solution)/shard_map/ppermute | solution.py:19
  96.6 3.3 collective-permute-done.3
  101.9 5.3 collective-permute-done.2
  121.6 46.3 %all-gather.3.cloned.1.call-done = bf16[1024,1024]{1,0:T(8,128)(2,1)} async-done(((bf16[16,1024]{1,0:T(8,128)(2,1)}), bf16[1024,1024]{1,0:T(8,128)(2,1)}) %all-gather.3.cloned.1.call-update) | async-done | bytes 2097168 | tf_op jit(solution)/shard_map/all_gather | solution.py:104
  167.9 4.4 copy.620
  172.3 3.2 fusion.5
  175.5 3.2 copy-done
  180.8 91.6 %all-gather.5.cloned.1.call-done = bf16[1024,1024]{1,0:T(8,128)(2,1)} async-done(((bf16[16,1024]{1,0:T(8,128)(2,1)}), bf16[1024,1024]{1,0:T(8,128)(2,1)}) %all-gather.5.cloned.1.call-update) | async-done | bytes 2097168 | tf_op jit(solution)/shard_map/all_gather | solution.py:105
  272.4 3.9 copy.664
  276.4 6.9 fusion
  285.3 4.2 multiply_reduce_fusion.7
  289.6 3.3 fusion.2
  294.8 3.4 bitcast_multiply_fusion.1
  298.2 5.4 copy.734
  303.8 6.3 multiply_convert_fusion
  313.7 2.2 fusion.59
  332.9 7.1 fusion.7
  340.0 5.3 copy.737
  360.9 5.2 multiply_convert_fusion.1
  376.2 2.3 fusion.64
  384.1 2.3 fusion.65
  420.8 16.6 %collective-permute-done.13 = bf16[2,128,1024]{2,1,0:T(8,128)(2,1)S(1)} collective-permute-done((bf16[2,128,1024]{2,1,0:T(8,128)(2,1)}, bf16[2,128,1024]{2,1,0:T(8,128)(2,1)S(1)}, u32[]{:S(2)}, u32[]{:S(2)}) %collective-permute-start.13) | collective-permute-done | bytes 524320 | tf_op jit(solution)/shard_map/ppermute | solution.py:19
  439.2 3.2 collective-permute-done.15
  442.4 3.2 fusion.67
  446.5 150.2 %reduce-scatter.3.cloned.1.call-done = f32[16,1024]{1,0:T(8,128)} async-done(((f32[1024,1024]{1,0:T(8,128)}), f32[16,1024]{1,0:T(8,128)}) %reduce-scatter.3.cloned.1.call-update) | async-done | bytes 65552 | tf_op jit(solution)/shard_map/reduce_scatter | solution.py:154
  598.2 286.7 %reduce-scatter.5.cloned.1.call-done = f32[16,1024]{1,0:T(8,128)} async-done(((f32[1024,1024]{1,0:T(8,128)}), f32[16,1024]{1,0:T(8,128)}) %reduce-scatter.5.cloned.1.call-update) | async-done | bytes 65552 | tf_op jit(solution)/shard_map/reduce_scatter | solution.py:155
  (273 shorter events, 139.1 us)
Async XLA Ops:
  7.2 160.7 %all-gather.3.cloned.1.call-start = ((), (), s32[]{:S(2)}) async-start(), calls=%async_computation.2 | async-start | bytes 2129920 | tf_op jit(solution)/shard_map/all_gather | solution.py:104
  7.9 264.5 %all-gather.5.cloned.1.call-start = ((), (), s32[]{:S(2)}) async-start(), calls=%async_computation.3 | async-start | bytes 2129920 | tf_op jit(solution)/shard_map/all_gather | solution.py:105
  11.0 40.8 %collective-permute-start.7 = (bf16[2,128,1024]{1,2,0:T(8,128)(2,1)}, bf16[2,128,1024]{1,2,0:T(8,128)(2,1)S(1)}, u32[]{:S(2)}, u32[]{:S(2)}) collective-permute-start(bf16[2,128,1024]{1,2,0:T(8,128)(2,1)} %pad_maximum_fusion), channel_id=1, source_target_pairs={{0,8},{1,9},{2,10},{3,11},{4,12},{5,13},{6,14},{7,15},{8,16},{9,17... | collective-permute-start | bytes 1572872 | tf_op jit(solution)/shard_map/ppermute | solution.py:19
  17.4 69.6 %collective-permute-start.6 = (bf16[2,128,1024]{1,2,0:T(8,128)(2,1)}, bf16[2,128,1024]{1,2,0:T(8,128)(2,1)}, u32[]{:S(2)}, u32[]{:S(2)}) collective-permute-start(bf16[2,128,1024]{1,2,0:T(8,128)(2,1)} %pad_maximum_fusion), channel_id=1, source_target_pairs={{0,7},{1,8},{2,9},{3,10},{4,11},{5,12},{6,13},{7,14},{8,15},{9,16}... | collective-permute-start | bytes 1572872 | tf_op jit(solution)/shard_map/ppermute | solution.py:19
  21.2 69.3 %collective-permute-start.5 = (bf16[2,128,1024]{1,2,0:T(8,128)(2,1)}, bf16[2,128,1024]{1,2,0:T(8,128)(2,1)}, u32[]{:S(2)}, u32[]{:S(2)}) collective-permute-start(bf16[2,128,1024]{1,2,0:T(8,128)(2,1)} %pad_maximum_fusion), channel_id=1, source_target_pairs={{0,6},{1,7},{2,8},{3,9},{4,10},{5,11},{6,12},{7,13},{8,14},{9,15},... | collective-permute-start | bytes 1572872 | tf_op jit(solution)/shard_map/ppermute | solution.py:19
  25.8 68.6 %collective-permute-start.4 = (bf16[2,128,1024]{1,2,0:T(8,128)(2,1)}, bf16[2,128,1024]{1,2,0:T(8,128)(2,1)}, u32[]{:S(2)}, u32[]{:S(2)}) collective-permute-start(bf16[2,128,1024]{1,2,0:T(8,128)(2,1)} %pad_maximum_fusion), channel_id=1, source_target_pairs={{0,5},{1,6},{2,7},{3,8},{4,9},{5,10},{6,11},{7,12},{8,13},{9,14},{... | collective-permute-start | bytes 1572872 | tf_op jit(solution)/shard_map/ppermute | solution.py:19
  30.6 69.3 %collective-permute-start.3 = (bf16[2,128,1024]{1,2,0:T(8,128)(2,1)}, bf16[2,128,1024]{1,2,0:T(8,128)(2,1)}, u32[]{:S(2)}, u32[]{:S(2)}) collective-permute-start(bf16[2,128,1024]{1,2,0:T(8,128)(2,1)} %pad_maximum_fusion), channel_id=1, source_target_pairs={{0,4},{1,5},{2,6},{3,7},{4,8},{5,9},{6,10},{7,11},{8,12},{9,13},{1... | collective-permute-start | bytes 1572872 | tf_op jit(solution)/shard_map/ppermute | solution.py:19
  32.7 564.0 %reduce-scatter.3.cloned.1.call-start = ((), (), s32[]{:S(2)}) async-start(), calls=%async_computation.4 | async-start | bytes 4259840 | tf_op jit(solution)/shard_map/reduce_scatter | solution.py:154
  37.0 20.1 %copy-start.34 = (bf16[128,8,128,1]{0,2,3,1:T(8,128)(2,1)}, bf16[128,8,128,1]{0,2,3,1:T(8,128)(2,1)S(1)}, u32[]{:S(2)}) copy-start(bf16[128,8,128,1]{0,2,3,1:T(8,128)(2,1)S(1)} %copy.760) | copy-start | bytes 786436
  40.6 67.9 %copy-start.52 = (pred[128,128]{0,1:T(8,128)(4,1)}, pred[128,128]{0,1:T(8,128)(4,1)S(1)}, u32[]{:S(2)}) copy-start(pred[128,128]{0,1:T(8,128)(4,1)S(1)} %get-tuple-element.85) | copy-start | bytes 49156
  40.6 70.7 %copy-start.54 = (pred[128,128]{0,1:T(8,128)(4,1)}, pred[128,128]{0,1:T(8,128)(4,1)S(1)}, u32[]{:S(2)}) copy-start(pred[128,128]{0,1:T(8,128)(4,1)S(1)} %get-tuple-element.87) | copy-start | bytes 49156
  41.4 134.1 %copy-start.32 = (pred[128,1024]{0,1:T(8,128)(4,1)}, pred[128,1024]{0,1:T(8,128)(4,1)S(1)}, u32[]{:S(2)}) copy-start(pred[128,1024]{0,1:T(8,128)(4,1)S(1)} %iota_compare_fusion) | copy-start | bytes 393220
  51.8 55.3 %collective-permute-start.2 = (bf16[2,128,1024]{1,2,0:T(8,128)(2,1)}, bf16[2,128,1024]{1,2,0:T(8,128)(2,1)S(1)}, u32[]{:S(2)}, u32[]{:S(2)}) collective-permute-start(bf16[2,128,1024]{1,2,0:T(8,128)(2,1)} %pad_maximum_fusion), channel_id=1, source_target_pairs={{0,3},{1,4},{2,5},{3,6},{4,7},{5,8},{6,9},{7,10},{8,11},{9,12},{10... | collective-permute-start | bytes 1572872 | tf_op jit(solution)/shard_map/ppermute | solution.py:19
  87.0 20.6 %collective-permute-start.1 = (bf16[2,128,1024]{1,2,0:T(8,128)(2,1)}, bf16[2,128,1024]{1,2,0:T(8,128)(2,1)S(1)}, u32[]{:S(2)}, u32[]{:S(2)}) collective-permute-start(bf16[2,128,1024]{1,2,0:T(8,128)(2,1)} %pad_maximum_fusion), channel_id=1, source_target_pairs={{0,2},{1,3},{2,4},{3,5},{4,6},{5,7},{6,8},{7,9},{8,10},{9,11},{10,... | collective-permute-start | bytes 1572872 | tf_op jit(solution)/shard_map/ppermute | solution.py:19
  90.5 17.2 %copy-start.3 = (f32[8,2,128,128]{2,3,1,0:T(8,128)}, f32[8,2,128,128]{2,3,1,0:T(8,128)S(1)}, u32[]{:S(2)}) copy-start(f32[8,2,128,128]{2,3,1,0:T(8,128)S(1)} %get-tuple-element.94) | copy-start | bytes 3145732
  90.5 19.0 %collective-permute-start = (bf16[2,128,1024]{1,2,0:T(8,128)(2,1)}, bf16[2,128,1024]{1,2,0:T(8,128)(2,1)S(1)}, u32[]{:S(2)}, u32[]{:S(2)}) collective-permute-start(bf16[2,128,1024]{1,2,0:T(8,128)(2,1)} %pad_maximum_fusion), channel_id=1, source_target_pairs={{0,1},{1,2},{2,3},{3,4},{4,5},{5,6},{6,7},{7,8},{8,9},{9,10},{10,1... | collective-permute-start | bytes 1572872 | tf_op jit(solution)/shard_map/ppermute | solution.py:19
  94.1 15.3 %copy-start.5 = (f32[8,2,128,128]{2,3,1,0:T(8,128)}, f32[8,2,128,128]{2,3,1,0:T(8,128)S(1)}, u32[]{:S(2)}) copy-start(f32[8,2,128,128]{2,3,1,0:T(8,128)S(1)} %get-tuple-element.96) | copy-start | bytes 3145732
  96.6 15.6 %copy-start.7 = (f32[8,2,128,128]{2,3,1,0:T(8,128)}, f32[8,2,128,128]{2,3,1,0:T(8,128)S(1)}, u32[]{:S(2)}) copy-start(f32[8,2,128,128]{2,3,1,0:T(8,128)S(1)} %get-tuple-element.98) | copy-start | bytes 3145732
  101.6 14.6 %copy-start.9 = (f32[8,2,128,128]{2,3,1,0:T(8,128)}, f32[8,2,128,128]{2,3,1,0:T(8,128)S(1)}, u32[]{:S(2)}) copy-start(f32[8,2,128,128]{2,3,1,0:T(8,128)S(1)} %get-tuple-element.100) | copy-start | bytes 3145732
  303.6 581.2 %reduce-scatter.5.cloned.1.call-start = ((), (), s32[]{:S(2)}) async-start(), calls=%async_computation.5 | async-start | bytes 4259840 | tf_op jit(solution)/shard_map/reduce_scatter | solution.py:155
  310.1 22.8 %copy-start.33 = (pred[128,1024]{0,1:T(8,128)(4,1)S(1)}, pred[128,1024]{0,1:T(8,128)(4,1)}, u32[]{:S(2)}) copy-start(pred[128,1024]{0,1:T(8,128)(4,1)} %copy-done.32) | copy-start | bytes 393220
  319.6 95.6 %collective-permute-start.8 = (bf16[2,128,1024]{2,1,0:T(8,128)(2,1)}, bf16[2,128,1024]{2,1,0:T(8,128)(2,1)}, u32[]{:S(2)}, u32[]{:S(2)}) collective-permute-start(bf16[2,128,1024]{2,1,0:T(8,128)(2,1)} %pad_maximum_fusion.1), channel_id=1, source_target_pairs={{1,0},{2,1},{3,2},{4,3},{5,4},{6,5},{7,6},{8,7},{9,8},{10,9},{11,1... | collective-permute-start | bytes 1572872 | tf_op jit(solution)/shard_map/ppermute | solution.py:19
  331.6 84.9 %collective-permute-start.9 = (bf16[2,128,1024]{2,1,0:T(8,128)(2,1)}, bf16[2,128,1024]{2,1,0:T(8,128)(2,1)}, u32[]{:S(2)}, u32[]{:S(2)}) collective-permute-start(bf16[2,128,1024]{2,1,0:T(8,128)(2,1)} %pad_maximum_fusion.2), channel_id=1, source_target_pairs={{2,0},{3,1},{4,2},{5,3},{6,4},{7,5},{8,6},{9,7},{10,8},{11,9},{12,... | collective-permute-start | bytes 1572872 | tf_op jit(solution)/shard_map/ppermute | solution.py:19
  351.9 66.0 %collective-permute-start.10 = (bf16[2,128,1024]{2,1,0:T(8,128)(2,1)}, bf16[2,128,1024]{2,1,0:T(8,128)(2,1)}, u32[]{:S(2)}, u32[]{:S(2)}) collective-permute-start(bf16[2,128,1024]{2,1,0:T(8,128)(2,1)} %pad_maximum_fusion.3), channel_id=1, source_target_pairs={{3,0},{4,1},{5,2},{6,3},{7,4},{8,5},{9,6},{10,7},{11,8},{12,9},{13... | collective-permute-start | bytes 1572872 | tf_op jit(solution)/shard_map/ppermute | solution.py:19
  359.6 61.2 %collective-permute-start.11 = (bf16[2,128,1024]{2,1,0:T(8,128)(2,1)}, bf16[2,128,1024]{2,1,0:T(8,128)(2,1)}, u32[]{:S(2)}, u32[]{:S(2)}) collective-permute-start(bf16[2,128,1024]{2,1,0:T(8,128)(2,1)} %pad_maximum_fusion.4), channel_id=1, source_target_pairs={{4,0},{5,1},{6,2},{7,3},{8,4},{9,5},{10,6},{11,7},{12,8},{13,9},{1... | collective-permute-start | bytes 1572872 | tf_op jit(solution)/shard_map/ppermute | solution.py:19
  372.5 48.3 %collective-permute-start.12 = (bf16[2,128,1024]{2,1,0:T(8,128)(2,1)}, bf16[2,128,1024]{2,1,0:T(8,128)(2,1)}, u32[]{:S(2)}, u32[]{:S(2)}) collective-permute-start(bf16[2,128,1024]{2,1,0:T(8,128)(2,1)} %pad_maximum_fusion.5), channel_id=1, source_target_pairs={{5,0},{6,1},{7,2},{8,3},{9,4},{10,5},{11,6},{12,7},{13,8},{14,9},{... | collective-permute-start | bytes 1572872 | tf_op jit(solution)/shard_map/ppermute | solution.py:19
  378.4 27.8 %copy-start.35 = (bf16[128,8,128,1]{0,2,3,1:T(8,128)(2,1)S(1)}, bf16[128,8,128,1]{0,2,3,1:T(8,128)(2,1)}, u32[]{:S(2)}) copy-start(bf16[128,8,128,1]{0,2,3,1:T(8,128)(2,1)} %copy-done.34) | copy-start | bytes 786436
  393.0 13.2 %copy-start.24 = (bf16[8,2,128,128]{2,3,1,0:T(8,128)(2,1)S(1)}, bf16[8,2,128,128]{2,3,1,0:T(8,128)(2,1)}, u32[]{:S(2)}) copy-start(bf16[8,2,128,128]{2,3,1,0:T(8,128)(2,1)} %get-tuple-element.79) | copy-start | bytes 1572868
  397.0 14.3 %copy-start.26 = (bf16[8,2,128,128]{2,3,1,0:T(8,128)(2,1)S(1)}, bf16[8,2,128,128]{2,3,1,0:T(8,128)(2,1)}, u32[]{:S(2)}) copy-start(bf16[8,2,128,128]{2,3,1,0:T(8,128)(2,1)} %get-tuple-element.75) | copy-start | bytes 1572868
  415.2 22.1 %collective-permute-start.13 = (bf16[2,128,1024]{2,1,0:T(8,128)(2,1)}, bf16[2,128,1024]{2,1,0:T(8,128)(2,1)S(1)}, u32[]{:S(2)}, u32[]{:S(2)}) collective-permute-start(bf16[2,128,1024]{2,1,0:T(8,128)(2,1)} %pad_maximum_fusion.6), channel_id=1, source_target_pairs={{6,0},{7,1},{8,2},{9,3},{10,4},{11,5},{12,6},{13,7},{14,8},{15,9},... | collective-permute-start | bytes 1572872 | tf_op jit(solution)/shard_map/ppermute | solution.py:19
  416.5 22.7 %collective-permute-start.14 = (bf16[2,128,1024]{2,1,0:T(8,128)(2,1)}, bf16[2,128,1024]{2,1,0:T(8,128)(2,1)}, u32[]{:S(2)}, u32[]{:S(2)}) collective-permute-start(bf16[2,128,1024]{2,1,0:T(8,128)(2,1)} %pad_maximum_fusion.7), channel_id=1, source_target_pairs={{7,0},{8,1},{9,2},{10,3},{11,4},{12,5},{13,6},{14,7},{15,8},{16,9}... | collective-permute-start | bytes 1572872 | tf_op jit(solution)/shard_map/ppermute | solution.py:19
  417.8 24.6 %collective-permute-start.15 = (bf16[2,128,1024]{2,1,0:T(8,128)(2,1)}, bf16[2,128,1024]{2,1,0:T(8,128)(2,1)}, u32[]{:S(2)}, u32[]{:S(2)}) collective-permute-start(bf16[2,128,1024]{2,1,0:T(8,128)(2,1)} %pad_maximum_fusion.8), channel_id=1, source_target_pairs={{8,0},{9,1},{10,2},{11,3},{12,4},{13,5},{14,6},{15,7},{16,8},{17,9... | collective-permute-start | bytes 1572872 | tf_op jit(solution)/shard_map/ppermute | solution.py:19
  (49 other events, 316.6 us)
Sparse Core Ops, SparseCore 0:
  9.7 158.1 all-gather.2
  169.6 102.7 all-gather.4
  303.7 292.9 reduce-scatter.2
  599.1 285.7 reduce-scatter.4
where the time goes:
time: 908 us; the launch traced here: 893 us
  waiting for transfers between devices  645 us (71%)
  matrix products  77.2 us (9%)
  local copies, waits for them, and re-layouts  70.4 us (8%)
  other arithmetic  43.8 us (5%)
  starting transfers between devices  41.7 us (5%)
  between operations  15.2 us (2%)
    reduce_scatter x1, waiting for transfers between devices, on_device(): lax.psum_scatter(tail_part[1], 'seq', scatter_dimension=0, tiled=True)  287 us
    reduce_scatter x1, waiting for transfers between devices, on_device(): lax.psum_scatter(tail_part[0], 'seq', scatter_dimension=0, tiled=True)  150 us
    all_gather x1, waiting for transfers between devices, on_device(): lax.all_gather(tail_values, 'seq', axis=0, tiled=True)  91.6 us
    ppermute x16, waiting for transfers between devices, passed_along(): lax.ppermute(value, axis, [(source, source + steps) for source in range(l...  69.3 us
    all_gather x1, waiting for transfers between devices, on_device(): lax.all_gather(tail_keys, 'seq', axis=0, tiled=True)  46.3 us
    ppermute x16, starting transfers between devices, passed_along(): lax.ppermute(value, axis, [(source, source + steps) for source in range(l...  41.4 us
    another operation x18, local copies, waits for them, and re-layouts, block_grads(): jnp.stack((key_grad, value_grad)).reshape(2, key_rows.shape[0], KVH * HD)  26.4 us
    dot_general x10, matrix products, block_grads(): jnp.einsum('kgrc,rkgd->ckd', rounded, dout_heads, preferred_element_type=...  22.9 us
  transfers between devices with their start and end apart: 20, of which 11 were waited for; matrix products, arithmetic and copies ran while one was open for 17% of the time, Pallas kernels for 0%

commit v1 on v0

v1 whole, which is shorter than its diff:
```python
import math

import jax
import jax.numpy as jnp
from jax import lax
from jax.experimental import pallas as pl
from jax.experimental.pallas import tpu as pltpu
from jax.sharding import PartitionSpec as P


KVH = 8
HD = 128
W = 1024
ROWS = 128
COHORT = 8
PAIR = 2 * HD
BAND = W + ROWS
STREAM = 2 * W
CHUNKS = BAND // ROWS
SCALE = 168.0 ** -0.5
SCALE2 = SCALE * math.log2(math.e)
NEG = -1.0e30
F32 = jnp.float32
BF16 = jnp.bfloat16
MESH = pl.DeviceIdType.MESH


def dot_nt(a, b):
    return lax.dot_general(a, b, (((1,), (1,)), ((), ())), preferred_element_type=F32)


def dot_nn(a, b):
    return jnp.dot(a, b, preferred_element_type=F32)


def at128(index, count=ROWS):
    return pl.ds(index * ROWS, count)


def kernel(len_ref, q_ref, do_ref, k_ref, v_ref, tk_ref, tv_ref,
           dq_ref, dk_ref, dv_ref, dtk_ref, dtv_ref,
           qb, dob, kv, tkv, kt, sc, dpc, ds, pr, acc, side, dqx,
           back, hsend, hrecv, osend, dqs, tsend, trecv, tfin,
           in_send, in_recv, halo_sem, tg_send, tg_recv,
           hg_send, hg_recv, tr_send, tr_recv, out_send, out_recv):
    me = lax.axis_index("seq")
    g = me // COHORT
    e = me % COHORT
    flip = 4 * (g % 2)
    h = (e + flip) % COHORT
    t0 = g * W

    def peer(t):
        return g * COHORT + (e + t) % COHORT

    def same_head(gg):
        return gg * COHORT + (h + 4 * (gg % 2)) % COHORT

    barrier = pltpu.get_barrier_semaphore()

    def greet(t, carry):
        pl.semaphore_signal(barrier, inc=1, device_id={"seq": peer(t)}, device_id_type=MESH)
        pl.semaphore_signal(barrier, inc=1, device_id={"seq": same_head((g + t) % COHORT)}, device_id_type=MESH)
        return carry

    lax.fori_loop(1, COHORT, greet, 0)
    pl.semaphore_wait(barrier, 2 * (COHORT - 1))

    left, right = pl.ds(0, HD), pl.ds(HD, HD)

    def placed(kind, head, source):
        tail_rows = pl.ds(pl.multiple_of(g * ROWS + source * 16, 16), 16)
        own = at128(COHORT + source)
        return (
            (k_ref.at[:, at128(head)], kv.at[own, left]),
            (v_ref.at[:, at128(head)], kv.at[own, right]),
            (tk_ref.at[:, at128(head)], tkv.at[tail_rows, left]),
            (tv_ref.at[:, at128(head)], tkv.at[tail_rows, right]),
            (q_ref.at[:, at128(2 * head, PAIR)], qb.at[at128(source), :]),
            (do_ref.at[:, at128(2 * head, PAIR)], dob.at[at128(source), :]),
        )[kind]

    def give(kind, t):
        to = (e + t) % COHORT
        src, dst = placed(kind, (to + flip) % COHORT, e)
        return pltpu.make_async_remote_copy(
            src_ref=src, dst_ref=dst, send_sem=in_send.at[kind, t], recv_sem=in_recv.at[kind, e],
            device_id={"seq": peer(t)}, device_id_type=MESH)

    def take(kind, t):
        source = (e + t) % COHORT
        src, dst = placed(kind, h, source)
        return pltpu.make_async_remote_copy(
            src_ref=src, dst_ref=dst, send_sem=in_send.at[kind, t], recv_sem=in_recv.at[kind, source],
            device_id={"seq": peer(t)}, device_id_type=MESH)

    def keep(kind):
        src, dst = placed(kind, h, e)
        return pltpu.make_async_copy(src, dst, in_recv.at[kind, e])

    def give_all(kinds):
        def body(t, carry):
            for kind in kinds:
                give(kind, t).start()
            return carry
        lax.fori_loop(1, COHORT, body, 0)
        for kind in kinds:
            keep(kind).start()

    def take_all(kinds):
        def body(t, carry):
            for kind in kinds:
                take(kind, t).wait_recv()
            return carry
        for kind in kinds:
            keep(kind).wait()
        lax.fori_loop(1, COHORT, body, 0)

    give_all((0, 1))
    give_all((2, 3))
    give_all((4, 5))

    take_all((0, 1))
    halo = pltpu.make_async_remote_copy(
        src_ref=kv.at[pl.ds(W, W), :], dst_ref=kv.at[pl.ds(0, W), :],
        send_sem=halo_sem.at[0], recv_sem=halo_sem.at[1],
        device_id={"seq": same_head((g + 1) % COHORT)}, device_id_type=MESH)
    halo.start()

    take_all((2, 3))

    def tail_give(t):
        return pltpu.make_async_remote_copy(
            src_ref=tkv.at[at128(g), :], dst_ref=tkv.at[at128(g), :],
            send_sem=tg_send.at[t], recv_sem=tg_recv.at[g],
            device_id={"seq": same_head((g + t) % COHORT)}, device_id_type=MESH)

    def tail_take(t):
        gg = (g + t) % COHORT
        return pltpu.make_async_remote_copy(
            src_ref=tkv.at[at128(gg), :], dst_ref=tkv.at[at128(gg), :],
            send_sem=tg_send.at[t], recv_sem=tg_recv.at[gg],
            device_id={"seq": same_head(gg)}, device_id_type=MESH)

    def start_tail(t, carry):
        tail_give(t).start()
        return carry

    def wait_tail(t, carry):
        tail_take(t).wait_recv()
        return carry

    lax.fori_loop(1, COHORT, start_tail, 0)
    lax.fori_loop(1, COHORT, wait_tail, 0)
    halo.wait_recv()

    @pl.when(g == 0)
    def _():
        kv[0:W, :] = tkv[...]

    first = len_ref[0]
    delta = first - t0
    whole = lax.shift_right_arithmetic(delta, 7)
    part = delta - whole * ROWS
    shift_row = lax.broadcasted_iota(jnp.int32, (ROWS, 2 * ROWS), 0)
    shift_col = lax.broadcasted_iota(jnp.int32, (ROWS, 2 * ROWS), 1)
    forth = (shift_col == shift_row + (ROWS - part)).astype(F32).astype(BF16)
    stream_row = lax.broadcasted_iota(jnp.int32, (ROWS, PAIR), 0)

    def second_stream(n, carry):
        low = jnp.clip(n - whole - 1, 0, COHORT - 1)
        high = jnp.clip(n - whole, 0, COHORT - 1)
        moved = (dot_nn(forth[:, :ROWS], tkv[at128(low), :])
                 + dot_nn(forth[:, ROWS:], tkv[at128(high), :]))
        plain = kv[at128(n), :]
        mixed = jnp.where(n * ROWS + stream_row < delta + W, moved, plain.astype(F32)).astype(BF16)
        kv[at128(16 + n), :] = mixed
        kt[:, at128(n)] = plain[:, :HD].T
        kt[:, at128(16 + n)] = mixed[:, :HD].T
        return carry

    lax.fori_loop(0, 16, second_stream, 0)

    take_all((4, 5))

    key_row = lax.broadcasted_iota(jnp.int32, (ROWS, PAIR), 0)
    query_row = lax.broadcasted_iota(jnp.int32, (ROWS, PAIR), 1) % ROWS
    lane_row = lax.broadcasted_iota(jnp.int32, (1, PAIR), 1) % ROWS

    def stacked(ref, block):
        rows = at128(block)
        return jnp.concatenate([ref[rows, :HD], ref[rows, HD:]], axis=0)

    def attend(block, start, valid):
        queries, douts = stacked(qb, block), stacked(dob, block)
        top = None
        for c in range(CHUNKS):
            logits = dot_nt(kv[at128(start + c), :HD], queries)
            if c == 0:
                logits = jnp.where(key_row > query_row, logits, NEG)
            if c == CHUNKS - 1:
                logits = jnp.where(key_row <= query_row, logits, NEG)
            sc[c * ROWS:(c + 1) * ROWS, :] = logits
            most = jnp.max(logits, axis=0, keepdims=True)
            top = most if top is None else jnp.maximum(top, most)
        total = jnp.zeros((1, PAIR), F32)
        mixed = jnp.zeros((1, PAIR), F32)
        for c in range(CHUNKS):
            rows = slice(c * ROWS, (c + 1) * ROWS)
            weight = jnp.exp2((sc[rows, :] - top) * SCALE2)
            dprob = dot_nt(kv[at128(start + c), HD:], douts)
            sc[rows, :] = weight
            dpc[rows, :] = dprob
            total = total + jnp.sum(weight, axis=0, keepdims=True)
            mixed = mixed + jnp.sum(weight * dprob, axis=0, keepdims=True)
        inverse = valid / total
        deltas = mixed / total
        for c in range(CHUNKS):
            rows = slice(c * ROWS, (c + 1) * ROWS)
            probs = sc[rows, :] * inverse
            pr[rows, :] = probs.astype(BF16)
            ds[rows, :] = (probs * (dpc[rows, :] - deltas)).astype(BF16)
        dq_t = dot_nn(kt[:, at128(start, BAND)], ds[...]) * SCALE
        return queries, douts, jnp.concatenate([dq_t[:, :HD].T, dq_t[:, HD:].T], axis=1)

    cut = jnp.clip(whole, 0, COHORT - 1)
    cut_row = lane_row + cut * ROWS
    in_cut = ((cut_row >= delta) & (cut * ROWS < delta)).astype(F32)
    queries, douts, dqx[...] = attend(cut, 16 + cut, in_cut)
    for c in range(CHUNKS):
        rows = slice(c * ROWS, (c + 1) * ROWS)
        side[rows, :HD] = dot_nn(ds[rows, :], queries)
        side[rows, HD:] = dot_nn(pr[rows, :], douts)

    def clear(n, carry):
        away = n - cut
        inside = ((away >= 0) & (away < CHUNKS)).astype(F32)
        acc[0, at128(n), :] = jnp.zeros((ROWS, PAIR), F32)
        acc[1, at128(n), :] = side[at128(jnp.clip(away, 0, CHUNKS - 1)), :] * inside
        return carry

    lax.fori_loop(0, 16, clear, 0)

    half = lax.broadcasted_iota(jnp.int32, (1, PAIR), 1)
    by_half = jnp.where(half < HD, SCALE, 1.0).astype(F32)

    def token_part(n):
        later = n * ROWS + stream_row >= delta + W
        return (acc[0, at128(n), :] + jnp.where(later, acc[1, at128(n), :], 0.0)) * by_half

    def send_dq(i):
        return pltpu.make_async_remote_copy(
            src_ref=dqs.at[at128(i), :], dst_ref=dq_ref.at[:, at128(2 * h, PAIR)],
            send_sem=out_send.at[0, i], recv_sem=out_recv.at[0, e],
            device_id={"seq": g * COHORT + i}, device_id_type=MESH)

    def send_halo_grad(i):
        return pltpu.make_async_remote_copy(
            src_ref=hsend.at[at128(i), :], dst_ref=hrecv.at[at128(i), :],
            send_sem=hg_send.at[i], recv_sem=hg_recv.at[i],
            device_id={"seq": same_head((g + COHORT - 1) % COHORT)}, device_id_type=MESH)

    has_halo = (g > 0).astype(F32)

    def main(i, carry):
        second = (i * ROWS >= delta).astype(jnp.int32)
        second_f = second.astype(F32)
        valid = jnp.maximum((lane_row + i * ROWS < delta).astype(F32), second_f)
        queries, douts, dq = attend(i, 16 * second + i, valid)
        for c in range(CHUNKS):
            rows = slice(c * ROWS, (c + 1) * ROWS)
            dkc = dot_nn(ds[rows, :], queries)
            dvc = dot_nn(pr[rows, :], douts)
            to = at128(i + c)
            acc[0, to, :HD] += dkc * (1.0 - second_f)
            acc[0, to, HD:] += dvc * (1.0 - second_f)
            acc[1, to, :HD] += dkc * second_f
            acc[1, to, HD:] += dvc * second_f
        dqs[at128(i), :] = (dq + dqx[...] * (cut == i).astype(F32)).astype(BF16)

        @pl.when(i != e)
        def _():
            send_dq(i).start()

        hsend[at128(i), :] = (token_part(i) * has_halo).astype(BF16)
        send_halo_grad(i).start()
        return carry

    lax.fori_loop(0, COHORT, main, 0)
    keep_dq = pltpu.make_async_copy(dqs.at[at128(e), :], dq_ref.at[:, at128(2 * h, PAIR)], out_recv.at[0, e])
    keep_dq.start()

    def tail_part(n, carry):
        earlier = n * ROWS + stream_row < delta + W
        back[at128(n), :] = jnp.where(earlier, acc[1, at128(n), :] * by_half, 0.0).astype(BF16)
        return carry

    lax.fori_loop(0, 16, tail_part, 0)

    def send_tail(n):
        return pltpu.make_async_remote_copy(
            src_ref=tsend.at[at128(n), :], dst_ref=trecv.at[at128(g), :],
            send_sem=tr_send.at[n], recv_sem=tr_recv.at[g],
            device_id={"seq": same_head(n)}, device_id_type=MESH)

    def take_tail(s):
        return pltpu.make_async_remote_copy(
            src_ref=tsend.at[at128(s), :], dst_ref=trecv.at[at128(s), :],
            send_sem=tr_send.at[s], recv_sem=tr_recv.at[s],
            device_id={"seq": same_head(s)}, device_id_type=MESH)

    is_first = (g == 0).astype(F32)

    def unmove(n, carry):
        low = n + whole
        high = low + 1
        low_in = (low >= 0) & (low < 16)
        high_in = (high >= 0) & (high < 16)
        hit = (shift_col == shift_row + part).astype(F32)
        low_hit = (hit[:, :ROWS] * low_in.astype(F32)).astype(BF16)
        high_hit = (hit[:, ROWS:] * high_in.astype(F32)).astype(BF16)
        moved = (dot_nn(low_hit, back[at128(jnp.clip(low, 0, 15)), :])
                 + dot_nn(high_hit, back[at128(jnp.clip(high, 0, 15)), :]))
        tsend[at128(n), :] = (moved + acc[0, at128(n), :] * by_half * is_first).astype(BF16)

        @pl.when(n != g)
        def _():
            send_tail(n).start()

        return carry

    lax.fori_loop(0, COHORT, unmove, 0)

    def send_own(n, kind):
        return pltpu.make_async_remote_copy(
            src_ref=osend.at[at128(n), (left, right)[kind]],
            dst_ref=(dk_ref, dv_ref)[kind].at[:, at128(h)],
            send_sem=out_send.at[1 + kind, n], recv_sem=out_recv.at[1 + kind, e],
            device_id={"seq": g * COHORT + n}, device_id_type=MESH)

    def own(n, carry):
        send_halo_grad(n).wait_recv()
        osend[at128(n), :] = (token_part(COHORT + n) + hrecv[at128(n), :].astype(F32)).astype(BF16)

        @pl.when(n != e)
        def _():
            send_own(n, 0).start()
            send_own(n, 1).start()

        return carry

    lax.fori_loop(0, COHORT, own, 0)

    def keep_own(kind):
        return pltpu.make_async_copy(
            osend.at[at128(e), (left, right)[kind]], (dk_ref, dv_ref)[kind].at[:, at128(h)], out_recv.at[1 + kind, e])

    keep_own(0).start()
    keep_own(1).start()

    def gather_tail(t, carry):
        take_tail((g + t) % COHORT).wait_recv()
        return carry

    lax.fori_loop(1, COHORT, gather_tail, 0)
    trecv[at128(g), :] = tsend[at128(g), :]
    summed = jnp.zeros((ROWS, PAIR), F32)
    for s in range(COHORT):
        summed = summed + trecv[s * ROWS:(s + 1) * ROWS, :].astype(F32)
    tfin[...] = summed.astype(BF16)

    def rows16(n):
        return pl.ds(pl.multiple_of(n * 16, 16), 16)

    def send_tail_out(t, kind):
        to = (e + t) % COHORT
        return pltpu.make_async_remote_copy(
            src_ref=tfin.at[rows16(to), (left, right)[kind]],
            dst_ref=(dtk_ref, dtv_ref)[kind].at[:, at128(h)],
            send_sem=out_send.at[3 + kind, to], recv_sem=out_recv.at[3 + kind, e],
            device_id={"seq": peer(t)}, device_id_type=MESH)

    def keep_tail_out(kind):
        return pltpu.make_async_copy(
            tfin.at[rows16(e), (left, right)[kind]], (dtk_ref, dtv_ref)[kind].at[:, at128(h)], out_recv.at[3 + kind, e])

    def start_tail_out(t, carry):
        send_tail_out(t, 0).start()
        send_tail_out(t, 1).start()
        return carry

    lax.fori_loop(1, COHORT, start_tail_out, 0)
    keep_tail_out(0).start()
    keep_tail_out(1).start()

    def finish(t, carry):
        source = (e + t) % COHORT
        head = (source + flip) % COHORT
        for kind in range(6):
            give(kind, t).wait_send()
        tail_give(t).wait_send()
        send_dq(source).wait_send()
        send_own(source, 0).wait_send()
        send_own(source, 1).wait_send()
        send_tail((g + t) % COHORT).wait_send()
        send_tail_out(t, 0).wait_send()
        send_tail_out(t, 1).wait_send()
        for kind, (src, dst) in enumerate((
            (dqs.at[at128(e), :], dq_ref.at[:, at128(2 * head, PAIR)]),
            (osend.at[at128(e), left], dk_ref.at[:, at128(head)]),
            (osend.at[at128(e), right], dv_ref.at[:, at128(head)]),
            (tfin.at[rows16(e), left], dtk_ref.at[:, at128(head)]),
            (tfin.at[rows16(e), right], dtv_ref.at[:, at128(head)]),
        )):
            pltpu.make_async_remote_copy(
                src_ref=src, dst_ref=dst, send_sem=out_send.at[kind, source], recv_sem=out_recv.at[kind, source],
                device_id={"seq": peer(t)}, device_id_type=MESH).wait_recv()
        return carry

    lax.fori_loop(1, COHORT, finish, 0)

    def finish_halo(i, carry):
        send_halo_grad(i).wait_send()
        return carry

    lax.fori_loop(0, COHORT, finish_halo, 0)
    halo.wait_send()
    keep_dq.wait()
    keep_own(0).wait()
    keep_own(1).wait()
    keep_tail_out(0).wait()
    keep_tail_out(1).wait()


def on_device(queries, keys, values, dout, tail_keys, tail_values, lengths):
    anywhere = pl.BlockSpec(memory_space=pl.ANY)
    dma = pltpu.SemaphoreType.DMA
    scratch = [
        pltpu.VMEM((W, PAIR), BF16),
        pltpu.VMEM((W, PAIR), BF16),
        pltpu.VMEM((2 * STREAM, PAIR), BF16),
        pltpu.VMEM((W, PAIR), BF16),
        pltpu.VMEM((HD, 2 * STREAM), BF16),
        pltpu.VMEM((BAND, PAIR), F32),
        pltpu.VMEM((BAND, PAIR), F32),
        pltpu.VMEM((BAND, PAIR), BF16),
        pltpu.VMEM((BAND, PAIR), BF16),
        pltpu.VMEM((2, STREAM, PAIR), F32),
        pltpu.VMEM((BAND, PAIR), F32),
        pltpu.VMEM((ROWS, PAIR), F32),
        pltpu.VMEM((STREAM, PAIR), BF16),
        pltpu.VMEM((W, PAIR), BF16),
        pltpu.VMEM((W, PAIR), BF16),
        pltpu.VMEM((W, PAIR), BF16),
        pltpu.VMEM((W, PAIR), BF16),
        pltpu.VMEM((W, PAIR), BF16),
        pltpu.VMEM((W, PAIR), BF16),
        pltpu.VMEM((ROWS, PAIR), BF16),
        dma((6, COHORT)), dma((6, COHORT)), dma((2,)), dma((COHORT,)), dma((COHORT,)),
        dma((COHORT,)), dma((COHORT,)), dma((COHORT,)), dma((COHORT,)), dma((5, COHORT)), dma((5, COHORT)),
    ]
    return pl.pallas_call(
        kernel,
        out_shape=(
            jax.ShapeDtypeStruct(queries.shape, BF16),
            jax.ShapeDtypeStruct(keys.shape, BF16),
            jax.ShapeDtypeStruct(values.shape, BF16),
            jax.ShapeDtypeStruct(tail_keys.shape, BF16),
            jax.ShapeDtypeStruct(tail_values.shape, BF16),
        ),
        in_specs=[pl.BlockSpec(memory_space=pltpu.SMEM)] + [anywhere] * 6,
        out_specs=(anywhere,) * 5,
        scratch_shapes=scratch,
        compiler_params=pltpu.CompilerParams(
            collective_id=0, has_side_effects=True, vmem_limit_bytes=48 * 1024 * 1024),
    )(lengths, queries, dout, keys, values, tail_keys, tail_values)


def solution(mesh):
    rows = P(("grp", "seq"), None)
    return jax.shard_map(
        on_device,
        mesh=mesh,
        in_specs=(rows,) * 6 + (P("grp"),),
        out_specs=(rows,) * 5,
        check_vma=False,
    )
```

time: 908 us -> 80.3 us (0.09); the launches traced: 893 us -> 79.7 us
  waiting for transfers between devices: 645 us -> 0 us
  matrix products: 77.2 us -> 0 us
  Pallas kernels: 0 us -> 69.5 us
  local copies, waits for them, and re-layouts: 70.4 us -> 9.57 us
  other arithmetic: 43.8 us -> 0 us
  starting transfers between devices: 41.7 us -> 0 us
  between operations: 15.2 us -> 0.66 us
    reduce_scatter x2 -> x0, waiting for transfers between devices: 437 us -> none  [the longest x1 287 us: on_device(): lax.psum_scatter(tail_part[1], 'seq', scatter_dimension=0, tiled=True)]
    all_gather x2 -> x0, waiting for transfers between devices: 138 us -> none  [the longest x1 91.6 us: on_device(): lax.all_gather(tail_values, 'seq', axis=0, tiled=True)]
    dot_general x50 -> x0, matrix products: 77.2 us -> none  [the longest x10 22.9 us: block_grads(): jnp.einsum('kgrc,rkgd->ckd', rounded, dout_heads, preferred_element_type=...]
    pallas_call x0 -> x1, Pallas kernels: none -> 69.5 us  [on_device(): pl.pallas_call(kernel, out_shape=(jax.ShapeDtypeStruct(queries.shape, BF1...]
    ppermute x16 -> x0, waiting for transfers between devices: 69.3 us -> none  [passed_along(): lax.ppermute(value, axis, [(source, source + steps) for source in range(l...]
    ppermute x16 -> x0, starting transfers between devices: 41.4 us -> none  [passed_along(): lax.ppermute(value, axis, [(source, source + steps) for source in range(l...]
    another operation x18 -> x0, local copies, waits for them, and re-layouts: 26.4 us -> none  [block_grads(): jnp.stack((key_grad, value_grad)).reshape(2, key_rows.shape[0], KVH * HD)]
    another operation x11 -> x0, other arithmetic: 19.1 us -> none  [the longest x8 14.2 us: block_grads(): jnp.stack((key_grad, value_grad)).reshape(2, key_rows.shape[0], KVH * HD)]
  transfers between devices with their start and end apart: 20 -> 0, of which waited for: 11 -> 0; matrix products, arithmetic and copies ran while one was open for 17% -> 0% of each run, Pallas kernels for 0% -> 0%
where the time goes in v1:
time: 80.3 us; the launch traced here: 79.7 us
  Pallas kernels  69.5 us (87%)
  local copies, waits for them, and re-layouts  9.57 us (12%)
    pallas_call x1, Pallas kernels, on_device(): pl.pallas_call(kernel, out_shape=(jax.ShapeDtypeStruct(queries.shape, BF1...  69.5 us
    unnamed x19, local copies, waits for them, and re-layouts  9.57 us

profile of v1, /device:TPU:1, one launch (start us, length us, event | category | flops | bytes accessed | tf_op | source)
XLA Modules:
  0.0 79.7 jit_solution(9174512394099205596)
XLA Ops:
  0.6 0.0 copy-start
  0.6 1.0 %copy-done = bf16[128,2048]{1,0:T(8,128)(2,1)S(1)} copy-done((bf16[128,2048]{1,0:T(8,128)(2,1)S(1)}, bf16[128,2048]{1,0:T(8,128)(2,1)}, u32[]{:S(2)}) %copy-start) | copy-done | bytes 524312
  1.7 0.0 copy-start.1
  1.7 1.0 %copy-done.1 = bf16[128,2048]{1,0:T(8,128)(2,1)S(1)} copy-done((bf16[128,2048]{1,0:T(8,128)(2,1)S(1)}, bf16[128,2048]{1,0:T(8,128)(2,1)}, u32[]{:S(2)}) %copy-start.1) | copy-done | bytes 524312
  2.7 0.0 copy-start.2
  2.7 0.9 %copy-done.2 = bf16[128,1024]{1,0:T(8,128)(2,1)S(1)} copy-done((bf16[128,1024]{1,0:T(8,128)(2,1)S(1)}, bf16[128,1024]{1,0:T(8,128)(2,1)}, u32[]{:S(2)}) %copy-start.2) | copy-done | bytes 262168
  3.7 0.0 copy-start.3
  3.7 0.9 %copy-done.3 = bf16[128,1024]{1,0:T(8,128)(2,1)S(1)} copy-done((bf16[128,1024]{1,0:T(8,128)(2,1)S(1)}, bf16[128,1024]{1,0:T(8,128)(2,1)}, u32[]{:S(2)}) %copy-start.3) | copy-done | bytes 262168
  4.6 0.0 copy-start.4
  4.6 0.8 copy-done.4
  5.4 0.0 copy-start.5
  5.4 0.8 copy-done.5
  6.1 0.0 copy-start.6
  6.1 0.7 copy-done.6
  6.8 69.5 %shard_map.110 = (bf16[128,2048]{1,0:T(8,128)(2,1)S(1)}, bf16[128,1024]{1,0:T(8,128)(2,1)S(1)}, bf16[128,1024]{1,0:T(8,128)(2,1)S(1)}, bf16[16,1024]{1,0:T(8,128)(2,1)S(1)}, bf16[16,1024]{1,0:T(8,128)(2,1)S(1)}) custom-call(s32[2]{0:T(128)S(1)} %copy-done.6, bf16[128,2048]{1,0:T(8,128)(2,1)S(1)} %copy-done, bf16[128,2048]{1,0:T(8,128)(2,1)S(1)} %copy-done.1, ...), custom_call_target="tpu_custom_call" | custom-call | tf_op jit(solution)/shard_map/pallas_call | solution.py:462
  76.3 0.8 copy.17
  77.1 0.7 copy.18
  77.8 0.7 copy.19
  78.5 0.6 copy.20
  79.1 0.6 copy.21
Async XLA Ops:
  0.6 1.0 %copy-start = (bf16[128,2048]{1,0:T(8,128)(2,1)S(1)}, bf16[128,2048]{1,0:T(8,128)(2,1)}, u32[]{:S(2)}) copy-start(bf16[128,2048]{1,0:T(8,128)(2,1)} %q_ref.1) | copy-start | bytes 1572868
  1.7 1.0 %copy-start.1 = (bf16[128,2048]{1,0:T(8,128)(2,1)S(1)}, bf16[128,2048]{1,0:T(8,128)(2,1)}, u32[]{:S(2)}) copy-start(bf16[128,2048]{1,0:T(8,128)(2,1)} %do_ref.1) | copy-start | bytes 1572868
  2.7 0.9 %copy-start.2 = (bf16[128,1024]{1,0:T(8,128)(2,1)S(1)}, bf16[128,1024]{1,0:T(8,128)(2,1)}, u32[]{:S(2)}) copy-start(bf16[128,1024]{1,0:T(8,128)(2,1)} %k_ref.1) | copy-start | bytes 786436
  3.7 0.9 %copy-start.3 = (bf16[128,1024]{1,0:T(8,128)(2,1)S(1)}, bf16[128,1024]{1,0:T(8,128)(2,1)}, u32[]{:S(2)}) copy-start(bf16[128,1024]{1,0:T(8,128)(2,1)} %v_ref.1) | copy-start | bytes 786436
  4.6 0.8 copy-start.4
  5.4 0.8 copy-start.5
  6.1 0.7 copy-start.6

commit v2 on v0

v2 whole, which is shorter than its diff:
```python
import math

import jax
import jax.numpy as jnp
from jax import lax
from jax.experimental import pallas as pl
from jax.experimental.pallas import tpu as pltpu
from jax.sharding import PartitionSpec as P


HD = 128
W = 1024
ROWS = 128
PLANE = 16
PLANES = 4
TOKENS = PLANE * ROWS
PAIR = 2 * HD
BLOCK = 256
BLOCKS = TOKENS // BLOCK
SLOTS = BLOCKS + 1
BAND = W + BLOCK
CHUNKS = BAND // ROWS
STREAM = W + TOKENS
UNITS = STREAM // BLOCK
HALO_UNITS = W // BLOCK
GROUP = 512
SCALE = 168.0 ** -0.5
SCALE2 = SCALE * math.log2(math.e)
NEG = -1.0e30
F32 = jnp.float32
BF16 = jnp.bfloat16
MESH = pl.DeviceIdType.MESH


def dot_nt(a, b):
    return lax.dot_general(a, b, (((1,), (1,)), ((), ())), preferred_element_type=F32)


def dot_nn(a, b):
    return jnp.dot(a, b, preferred_element_type=F32)


def at128(index, count=ROWS):
    return pl.ds(index * ROWS, count)


def at256(index, count=BLOCK):
    return pl.ds(index * BLOCK, count)


def at16(index):
    return pl.ds(pl.multiple_of(index * 16, 16), 16)


def kernel(len_ref, q_ref, do_ref, k_ref, v_ref, tk_ref, tv_ref,
           dq_ref, dk_ref, dv_ref, dtk_ref, dtv_ref,
           qb, dob, kv, tkv, kt, sc, dpc, ds, pr, dsx, prx, qq, oo, dqx,
           tok, back, first_part, xsend, xrecv, hsend, hrecv, osend, dqs,
           txs, txr, tsend, trecv, tfin,
           in_send, in_recv, tg_send, tg_recv, ts_send, ts_recv, halo_send, halo_recv, sh_send, sh_recv,
           x_send, x_recv, hg_send, hg_recv, tx_send, tx_recv, tr_send, tr_recv, out_send, out_recv):
    me = lax.axis_index("seq")
    p = me // PLANE
    e = me % PLANE
    head = e // 2
    core = e % 2
    t0 = p * TOKENS
    mine = pl.ds(core * HD, HD)
    other = pl.ds((1 - core) * HD, HD)
    sibling = me + 1 - 2 * core

    def peer(t):
        return p * PLANE + (e + t) % PLANE

    def in_plane(pp):
        return pp * PLANE + e

    def remote(src, dst, send_sem, recv_sem, device):
        return pltpu.make_async_remote_copy(
            src_ref=src, dst_ref=dst, send_sem=send_sem, recv_sem=recv_sem,
            device_id={"seq": device}, device_id_type=MESH)

    barrier = pltpu.get_barrier_semaphore()

    def greet(t, carry):
        pl.semaphore_signal(barrier, inc=1, device_id={"seq": peer(t)}, device_id_type=MESH)
        return carry

    def greet_plane(t, carry):
        pl.semaphore_signal(barrier, inc=1, device_id={"seq": in_plane((p + t) % PLANES)}, device_id_type=MESH)
        return carry

    lax.fori_loop(1, PLANE, greet, 0)
    lax.fori_loop(1, PLANES, greet_plane, 0)
    pl.semaphore_wait(barrier, PLANE + PLANES - 2)

    def origin(kind, to, role):
        if kind == 0:
            return (tk_ref, tv_ref)[role].at[:, at128(to // 2)]
        if kind == 1:
            return (k_ref, v_ref)[role].at[:, at128(to // 2)]
        return (q_ref, do_ref)[kind - 2].at[:, at128(to)]

    def target(kind, source, role):
        columns = pl.ds(role * HD, HD)
        if kind == 0:
            return tkv.at[at16(p * PLANE + source), columns]
        if kind == 1:
            return kv.at[at128(W // ROWS + source), columns]
        return (qb, dob)[kind - 2].at[at128(source), :]

    def give(kind, t, role):
        to = (e + t) % PLANE
        return remote(origin(kind, to, role), target(kind, e, to % 2),
                      in_send.at[kind, t], in_recv.at[kind, e], peer(t))

    def take(kind, source):
        return remote(origin(kind, e, 0), target(kind, source, core),
                      in_send.at[kind, 0], in_recv.at[kind, source], sibling)

    def keep(kind, role):
        return pltpu.make_async_copy(origin(kind, e, role), target(kind, e, core), in_recv.at[kind, e])

    def by_role(kind, to, act):
        if kind >= 2:
            act(0)
        else:
            for role in range(2):
                @pl.when(to % 2 == role)
                def _(role=role):
                    act(role)

    def give_all(kind):
        def body(t, carry):
            by_role(kind, (e + t) % PLANE, lambda role: give(kind, t, role).start())
            return carry
        lax.fori_loop(1, PLANE, body, 0)
        by_role(kind, e, lambda role: keep(kind, role).start())

    def take_some(kind, low, high):
        def body(source, carry):
            @pl.when(source == e)
            def _():
                keep(kind, 0).wait()

            @pl.when(source != e)
            def _():
                take(kind, source).wait_recv()

            return carry
        lax.fori_loop(low, high, body, 0)

    def tail_give(t):
        rows = at256(p)
        return remote(tkv.at[rows, mine], tkv.at[rows, mine], tg_send.at[t], tg_recv.at[p], in_plane((p + t) % PLANES))

    def tail_take(pp):
        rows = at256(pp)
        return remote(tkv.at[rows, mine], tkv.at[rows, mine], tg_send.at[0], tg_recv.at[pp], in_plane(pp))

    def tail_share(pp):
        rows = at256(pp)
        return remote(tkv.at[rows, mine], tkv.at[rows, mine], ts_send.at[pp], ts_recv.at[pp], sibling)

    def tail_shared(pp):
        rows = at256(pp)
        return remote(tkv.at[rows, mine], tkv.at[rows, other], ts_send.at[pp], ts_recv.at[pp], sibling)

    def halo(k):
        return remote(kv.at[pl.ds(TOKENS + k * GROUP, GROUP), mine], kv.at[pl.ds(k * GROUP, GROUP), mine],
                      halo_send.at[k], halo_recv.at[k], in_plane((p + 1) % PLANES))

    def share(k):
        rows = pl.ds(k * GROUP, GROUP)
        return remote(kv.at[rows, mine], kv.at[rows, mine], sh_send.at[k], sh_recv.at[k], sibling)

    def shared(k):
        rows = pl.ds(k * GROUP, GROUP)
        return remote(kv.at[rows, mine], kv.at[rows, other], sh_send.at[k], sh_recv.at[k], sibling)

    give_all(0)
    give_all(1)
    give_all(2)
    give_all(3)

    take_some(0, 0, PLANE)
    for t in range(1, PLANES):
        tail_give(t).start()
    tail_share(p).start()

    for k in (5, 4, 3, 2):
        take_some(1, 4 * (k - 2), 4 * (k - 1))
        if k >= 4:
            halo(k - 4).start()
        share(k).start()

    edge = jnp.zeros((BLOCK, BLOCK), BF16)
    for ref in (dsx, prx):
        for n in range(19):
            if not 7 <= n < 12:
                ref[n * BLOCK:(n + 1) * BLOCK, :] = edge

    def wait_tail(t, carry):
        pp = (p + t) % PLANES
        tail_take(pp).wait_recv()
        tail_share(pp).start()
        return carry

    lax.fori_loop(1, PLANES, wait_tail, 0)

    def wait_shared_tail(pp, carry):
        tail_shared(pp).wait_recv()
        return carry

    lax.fori_loop(0, PLANES, wait_shared_tail, 0)

    first = len_ref[0]
    delta = first - t0
    whole = lax.shift_right_arithmetic(delta, 7)
    part = delta - whole * ROWS
    shift_row = lax.broadcasted_iota(jnp.int32, (ROWS, 2 * ROWS), 0)
    shift_col = lax.broadcasted_iota(jnp.int32, (ROWS, 2 * ROWS), 1)
    forth = (shift_col == shift_row + (ROWS - part)).astype(F32).astype(BF16)
    stream_row = lax.broadcasted_iota(jnp.int32, (ROWS, PAIR), 0)

    def second_stream(n, carry):
        low = jnp.clip(n - whole - 1, 0, W // ROWS - 1)
        high = jnp.clip(n - whole, 0, W // ROWS - 1)
        moved = (dot_nn(forth[:, :ROWS], tkv[at128(low), :])
                 + dot_nn(forth[:, ROWS:], tkv[at128(high), :]))
        plain = kv[at128(n), :]
        mixed = jnp.where(n * ROWS + stream_row < delta + W, moved, plain.astype(F32)).astype(BF16)
        kv[at128(STREAM // ROWS + n), :] = mixed
        kt[:, at128(n)] = plain[:, :HD].T
        kt[:, at128(STREAM // ROWS + n)] = mixed[:, :HD].T
        return carry

    for k in (5, 4, 3, 2):
        shared(k).wait_recv()
        lax.fori_loop(4 * k, 4 * k + 4, second_stream, 0)

    for k in (1, 0):
        halo(k).wait_recv()
        share(k).start()
        shared(k).wait_recv()
        share(k).wait_send()

        @pl.when(p == 0)
        def _(k=k):
            kv[k * GROUP:(k + 1) * GROUP, :] = tkv[k * GROUP:(k + 1) * GROUP, :]

        lax.fori_loop(4 * k, 4 * k + 4, second_stream, 0)

    key_row = lax.broadcasted_iota(jnp.int32, (ROWS, BLOCK), 0)
    query_row = lax.broadcasted_iota(jnp.int32, (ROWS, BLOCK), 1)
    lane_row = lax.broadcasted_iota(jnp.int32, (1, BLOCK), 1)
    cut = jnp.clip(lax.shift_right_arithmetic(delta, 8), 0, BLOCKS - 1)

    def is_second(i):
        return (i * BLOCK >= delta).astype(jnp.int32)

    def band(block, second, c):
        return at128(2 * block + c + second * (STREAM // ROWS))

    take_some(2, 0, PLANE)

    def slot_place(slot):
        if slot == BLOCKS:
            return cut, jnp.int32(1)
        return slot, is_second(slot)

    def logits_of(slot):
        block, second = slot_place(slot)
        queries = qb[at256(block), :]
        rows = at256(slot)
        qq[rows, :HD] = queries * (1 - second).astype(F32).astype(BF16)
        qq[rows, HD:] = queries * second.astype(F32).astype(BF16)
        top = None
        for c in range(CHUNKS):
            logits = dot_nt(kv[band(block, second, c), :HD], queries)
            if c < 2:
                logits = jnp.where(key_row + c * ROWS > query_row, logits, NEG)
            if c >= CHUNKS - 2:
                logits = jnp.where(key_row + (c * ROWS - W) <= query_row, logits, NEG)
            sc[slot, c * ROWS:(c + 1) * ROWS, :] = logits
            most = jnp.max(logits, axis=0, keepdims=True)
            top = most if top is None else jnp.maximum(top, most)
        return top

    def weigh(slot, top):
        total = jnp.zeros((1, BLOCK), F32)
        for c in range(CHUNKS):
            weight = jnp.exp2((sc[slot, c * ROWS:(c + 1) * ROWS, :] - top) * SCALE2)
            sc[slot, c * ROWS:(c + 1) * ROWS, :] = weight
            total = total + jnp.sum(weight, axis=0, keepdims=True)
        return total

    order = [BLOCKS] + list(range(BLOCKS))
    totals = {}
    tops = {order[0]: logits_of(order[0])}
    for at, slot in enumerate(order):
        if at + 1 < SLOTS:
            tops[order[at + 1]] = logits_of(order[at + 1])
        totals[slot] = weigh(slot, tops[slot])

    take_some(3, 0, PLANE)

    cut_row = lane_row + cut * BLOCK
    in_cut = ((cut_row >= delta) & (cut * BLOCK < delta)).astype(F32)
    inner = 7 * BLOCK

    def turn(slot):
        return 0 if slot == BLOCKS else (slot + 1) % 2

    def dprobs_of(slot):
        block, second = slot_place(slot)
        douts = dob[at256(block), :]
        rows = at256(slot)
        oo[rows, :HD] = douts * (1 - second).astype(F32).astype(BF16)
        oo[rows, HD:] = douts * second.astype(F32).astype(BF16)
        mixed = jnp.zeros((1, BLOCK), F32)
        for c in range(CHUNKS):
            rows = slice(c * ROWS, (c + 1) * ROWS)
            dprob = dot_nt(kv[band(block, second, c), HD:], douts)
            dpc[turn(slot), rows, :] = dprob
            mixed = mixed + jnp.sum(sc[slot, rows, :] * dprob, axis=0, keepdims=True)
        return mixed

    def scores(slot, mixed):
        if slot == BLOCKS:
            valid = in_cut
        else:
            valid = jnp.maximum((lane_row + slot * BLOCK < delta).astype(F32), is_second(slot).astype(F32))
        inverse = valid / totals[slot]
        deltas = mixed / totals[slot]
        for c in range(CHUNKS):
            rows = slice(c * ROWS, (c + 1) * ROWS)
            probs = sc[slot, rows, :] * inverse
            dscores = (probs * (dpc[turn(slot), rows, :] - deltas)).astype(BF16)
            if slot == BLOCKS:
                rows = slice(inner + c * ROWS, inner + (c + 1) * ROWS)
                prx[rows, :] = probs.astype(BF16)
                dsx[rows, :] = dscores
            else:
                pr[slot, rows, :] = probs.astype(BF16)
                ds[slot, rows, :] = dscores

    def query_grad(slot):
        block, second = slot_place(slot)
        keys_t = kt[:, pl.ds(2 * block * ROWS + second * STREAM, BAND)]
        if slot == BLOCKS:
            dqx[...] = (dot_nn(keys_t, dsx[inner:inner + BAND, :]) * SCALE).T
            return
        dq = (dot_nn(keys_t, ds[slot]) * SCALE).T
        dqs[at256(slot), :] = (dq + dqx[...] * (cut == slot).astype(F32)).astype(BF16)

    def send_dq(n):
        return remote(dqs.at[at128(n), :], dq_ref.at[:, at128(e)], out_send.at[0, n], out_recv.at[0, e], p * PLANE + n)

    def swap(u):
        return remote(xsend.at[at256(u), other], xrecv.at[at256(u), :], x_send.at[u], x_recv.at[u], sibling)

    def send_halo_grad(u):
        return remote(hsend.at[at256(u), :], hrecv.at[at256(u), :], hg_send.at[u], hg_recv.at[u],
                      in_plane((p + PLANES - 1) % PLANES))

    def send_own(n, role):
        return remote(osend.at[at128(n), :], (dk_ref, dv_ref)[role].at[:, at128(head)],
                      out_send.at[1, n], out_recv.at[1 + role, head], p * PLANE + n)

    def keep_dq():
        return pltpu.make_async_copy(dqs.at[at128(e), :], dq_ref.at[:, at128(e)], out_recv.at[0, e])

    def keep_own(role):
        return pltpu.make_async_copy(
            osend.at[at128(e), :], (dk_ref, dv_ref)[role].at[:, at128(head)], out_recv.at[1 + role, head])

    has_halo = (p > 0).astype(F32)
    is_first = (p == 0).astype(F32)
    unit_row = lax.broadcasted_iota(jnp.int32, (BLOCK, HD), 0)

    def send_some_dq(n, carry):
        @pl.when(n != e)
        def _():
            send_dq(n).start()

        return carry

    def gather(u):
        low, high = max(0, u - 4), min(BLOCKS - 1, u)
        extra = at256(u + 7 - cut)
        later = u * BLOCK + unit_row >= delta + W
        token = []
        for ref, ref_x, right_side, scale in ((ds, dsx, qq, SCALE), (pr, prx, oo, 1.0)):
            parts = [ref[i, (u - i) * BLOCK:(u - i + 1) * BLOCK, :] for i in range(low, high + 1)]
            both = dot_nn(jnp.concatenate(parts, axis=1), right_side[low * BLOCK:(high + 1) * BLOCK, :])
            both = (both + dot_nn(ref_x[extra, :], right_side[BLOCKS * BLOCK:, :])) * scale
            token.append(both[:, :HD] + jnp.where(later, both[:, HD:], 0.0))
        rows = slice(u * BLOCK, (u + 1) * BLOCK)
        token = jnp.concatenate(token, axis=1)
        tok[u % 4] = token
        xsend[rows, :] = token.astype(BF16)
        swap(u).start()
        if u < HALO_UNITS:
            first_part[rows, :] = (token * is_first).astype(BF16)

    def settle(u):
        swap(u).wait_recv()
        total = tok[u % 4, :, mine] + xrecv[u * BLOCK:(u + 1) * BLOCK, :].astype(F32)
        if u < HALO_UNITS:
            hsend[u * BLOCK:(u + 1) * BLOCK, :] = (total * has_halo).astype(BF16)
            send_halo_grad(u).start()
            return
        v = u - HALO_UNITS
        if v >= BLOCKS - HALO_UNITS:
            w = v - (BLOCKS - HALO_UNITS)
            send_halo_grad(w).wait_recv()
            total = total + hrecv[w * BLOCK:(w + 1) * BLOCK, :].astype(F32)
        osend[v * BLOCK:(v + 1) * BLOCK, :] = total.astype(BF16)
        for n in (2 * v, 2 * v + 1):
            for role in range(2):
                @pl.when((n != e) & (core == role))
                def _(n=n, role=role):
                    send_own(n, role).start()

    base = lax.shift_right_arithmetic(delta, 8)
    lag = delta - base * BLOCK
    back_row = lax.broadcasted_iota(jnp.int32, (BLOCK, 2 * BLOCK), 0)
    back_col = lax.broadcasted_iota(jnp.int32, (BLOCK, 2 * BLOCK), 1)

    def tail_unit(k):
        token = []
        early = (base + k) * BLOCK + unit_row < delta + W
        for ref, ref_x, right_side, scale in ((ds, dsx, qq, SCALE), (pr, prx, oo, 1.0)):
            lefts = [ref_x[inner + k * BLOCK:inner + (k + 1) * BLOCK, :]]
            rights = [right_side[BLOCKS * BLOCK:, HD:]]
            for d in range(k + 1):
                slot = base + d
                inside = ((slot >= 0) & (slot < BLOCKS)).astype(F32).astype(BF16)
                slot = jnp.clip(slot, 0, BLOCKS - 1)
                lefts.append(ref[slot, (k - d) * BLOCK:(k - d + 1) * BLOCK, :])
                rights.append(right_side[at256(slot), HD:] * inside)
            token.append(jnp.where(early, dot_nn(jnp.concatenate(lefts, axis=1), jnp.concatenate(rights, axis=0)) * scale, 0.0))
        back[k * BLOCK:(k + 1) * BLOCK, :] = jnp.concatenate(token, axis=1).astype(BF16)

    def swap_tail(pp):
        return remote(txs.at[at256(pp), other], txr.at[at256(pp), :], tx_send.at[pp], tx_recv.at[pp], sibling)

    def send_tail(pp):
        return remote(tsend.at[at256(pp), :], trecv.at[at256(p), :], tr_send.at[pp], tr_recv.at[p], in_plane(pp))

    def take_tail(pp):
        return remote(tsend.at[at256(pp), :], trecv.at[at256(pp), :], tr_send.at[pp], tr_recv.at[pp], in_plane(pp))

    def start_tail_sums():
        for k in range(W // BLOCK + 1):
            tail_unit(k)
        hit = (back_col == back_row + lag).astype(F32).astype(BF16)
        for pp in range(PLANES):
            rows = slice(pp * BLOCK, (pp + 1) * BLOCK)
            moved = dot_nn(hit, back[pp * BLOCK:(pp + 2) * BLOCK, :])
            txs[rows, :] = (moved + first_part[rows, :].astype(F32)).astype(BF16)
        for pp in range(PLANES):
            swap_tail(pp).start()

    def send_tail_sums():
        for pp in range(PLANES):
            swap_tail(pp).wait_recv()
        for pp in range(PLANES):
            rows = slice(pp * BLOCK, (pp + 1) * BLOCK)
            tsend[rows, :] = (txs[rows, mine].astype(F32) + txr[rows, :].astype(F32)).astype(BF16)
        for pp in range(PLANES):
            @pl.when(p != pp)
            def _(pp=pp):
                send_tail(pp).start()

    mixes = {order[0]: dprobs_of(order[0])}
    for at, slot in enumerate(order):
        if at + 1 < SLOTS:
            mixes[order[at + 1]] = dprobs_of(order[at + 1])
        scores(slot, mixes[slot])
        if at > 0:
            query_grad(order[at - 1])
        if slot in (2, 4, 6):
            lax.fori_loop(2 * slot - 4, 2 * slot, send_some_dq, 0)
        if slot == 3:
            for u in range(4):
                gather(u)
        if slot == 5:
            for u in range(4):
                settle(u)
    query_grad(BLOCKS - 1)
    start_tail_sums()
    lax.fori_loop(12, PLANE, send_some_dq, 0)
    gather(4)
    gather(5)
    send_tail_sums()
    for u in range(6, UNITS):
        gather(u)
        settle(u - 2)
    settle(UNITS - 2)
    keep_dq().start()

    settle(UNITS - 1)
    for role in range(2):
        @pl.when(core == role)
        def _(role=role):
            keep_own(role).start()

    summed = tsend[at256(p), :].astype(F32)
    for t in range(1, PLANES):
        pp = (p + t) % PLANES
        take_tail(pp).wait_recv()
        summed = summed + trecv[at256(pp), :].astype(F32)
    tfin[...] = summed.astype(BF16)

    def send_tail_out(t, role):
        to = (e + t) % PLANE
        return remote(tfin.at[at16(to), :], (dtk_ref, dtv_ref)[role].at[:, at128(head)],
                      out_send.at[2, to], out_recv.at[3 + role, head], peer(t))

    def keep_tail_out(role):
        return pltpu.make_async_copy(
            tfin.at[at16(e), :], (dtk_ref, dtv_ref)[role].at[:, at128(head)], out_recv.at[3 + role, head])

    def start_tail_out(t, carry):
        for role in range(2):
            @pl.when(core == role)
            def _(role=role):
                send_tail_out(t, role).start()
        return carry

    lax.fori_loop(1, PLANE, start_tail_out, 0)
    for role in range(2):
        @pl.when(core == role)
        def _(role=role):
            keep_tail_out(role).start()

    def finish_sends(t, carry):
        n = (e + t) % PLANE
        for kind in range(4):
            give(kind, t, 0).wait_send()
        send_dq(n).wait_send()
        send_own(n, 0).wait_send()
        send_tail_out(t, 0).wait_send()
        remote(dqs.at[at128(e), :], dq_ref.at[:, at128(n)], out_send.at[0, n], out_recv.at[0, n], peer(t)).wait_recv()
        return carry

    lax.fori_loop(1, PLANE, finish_sends, 0)

    def finish_units(u, carry):
        swap(u).wait_send()
        return carry

    lax.fori_loop(0, UNITS, finish_units, 0)

    def finish_halo(k, carry):
        halo(k).wait_send()
        return carry

    lax.fori_loop(0, 2, finish_halo, 0)

    def finish_share(k, carry):
        share(k).wait_send()
        return carry

    lax.fori_loop(2, 6, finish_share, 0)

    def finish_planes(pp, carry):
        send_halo_grad(pp).wait_send()
        tail_share(pp).wait_send()
        swap_tail(pp).wait_send()

        @pl.when(p != pp)
        def _():
            send_tail(pp).wait_send()

        return carry

    lax.fori_loop(0, PLANES, finish_planes, 0)
    for t in range(1, PLANES):
        tail_give(t).wait_send()
    keep_dq().wait()

    def finish_heads(n, carry):
        columns = at128(n)
        for role in range(2):
            @pl.when((n == head) & (core == role))
            def _(role=role):
                keep_own(role).wait()
                keep_tail_out(role).wait()

            @pl.when((n != head) | (core != role))
            def _(role=role):
                remote(osend.at[at128(e), :], (dk_ref, dv_ref)[role].at[:, columns],
                       out_send.at[1, 0], out_recv.at[1 + role, n], sibling).wait_recv()
                remote(tfin.at[at16(e), :], (dtk_ref, dtv_ref)[role].at[:, columns],
                       out_send.at[2, 0], out_recv.at[3 + role, n], sibling).wait_recv()

        return carry

    lax.fori_loop(0, PLANE // 2, finish_heads, 0)


def write_out(*refs):
    for source, target in zip(refs[:5], refs[5:]):
        target[...] = source[...]


def on_device(queries, keys, values, dout, tail_keys, tail_values, lengths):
    anywhere = pl.BlockSpec(memory_space=pl.ANY)
    dma = pltpu.SemaphoreType.DMA
    scratch = [
        pltpu.VMEM((TOKENS, HD), BF16),
        pltpu.VMEM((TOKENS, HD), BF16),
        pltpu.VMEM((2 * STREAM, PAIR), BF16),
        pltpu.VMEM((W, PAIR), BF16),
        pltpu.VMEM((HD, 2 * STREAM), BF16),
        pltpu.VMEM((SLOTS, BAND, BLOCK), F32),
        pltpu.VMEM((2, BAND, BLOCK), F32),
        pltpu.VMEM((BLOCKS, BAND, BLOCK), BF16),
        pltpu.VMEM((BLOCKS, BAND, BLOCK), BF16),
        pltpu.VMEM((19 * BLOCK, BLOCK), BF16),
        pltpu.VMEM((19 * BLOCK, BLOCK), BF16),
        pltpu.VMEM((SLOTS * BLOCK, PAIR), BF16),
        pltpu.VMEM((SLOTS * BLOCK, PAIR), BF16),
        pltpu.VMEM((BLOCK, HD), F32),
        pltpu.VMEM((4, BLOCK, PAIR), F32),
        pltpu.VMEM((W + BLOCK, PAIR), BF16),
        pltpu.VMEM((W, PAIR), BF16),
        pltpu.VMEM((STREAM, PAIR), BF16),
        pltpu.VMEM((STREAM, HD), BF16),
        pltpu.VMEM((W, HD), BF16),
        pltpu.VMEM((W, HD), BF16),
        pltpu.VMEM((TOKENS, HD), BF16),
        pltpu.VMEM((TOKENS, HD), BF16),
        pltpu.VMEM((W, PAIR), BF16),
        pltpu.VMEM((W, HD), BF16),
        pltpu.VMEM((W, HD), BF16),
        pltpu.VMEM((W, HD), BF16),
        pltpu.VMEM((BLOCK, HD), BF16),
        dma((4, PLANE)), dma((4, PLANE)),
        dma((PLANES,)), dma((PLANES,)), dma((PLANES,)), dma((PLANES,)),
        dma((2,)), dma((2,)), dma((6,)), dma((6,)),
        dma((UNITS,)), dma((UNITS,)), dma((PLANES,)), dma((PLANES,)),
        dma((PLANES,)), dma((PLANES,)), dma((PLANES,)), dma((PLANES,)),
        dma((3, PLANE)), dma((5, PLANE)),
    ]
    grads = pl.pallas_call(
        kernel,
        out_shape=(
            jax.ShapeDtypeStruct(queries.shape, BF16),
            jax.ShapeDtypeStruct(keys.shape, BF16),
            jax.ShapeDtypeStruct(values.shape, BF16),
            jax.ShapeDtypeStruct(tail_keys.shape, BF16),
            jax.ShapeDtypeStruct(tail_values.shape, BF16),
        ),
        in_specs=[pl.BlockSpec(memory_space=pltpu.SMEM)] + [anywhere] * 6,
        out_specs=(anywhere,) * 5,
        scratch_shapes=scratch,
        compiler_params=pltpu.CompilerParams(
            collective_id=0, has_side_effects=True, vmem_limit_bytes=62 * 1024 * 1024),
    )(lengths, queries, dout, keys, values, tail_keys, tail_values)
    return pl.pallas_call(
        write_out,
        out_shape=tuple(jax.ShapeDtypeStruct(x.shape, x.dtype) for x in grads),
    )(*grads)


def solution(mesh):
    rows = P(("grp", "seq"), None)
    return jax.shard_map(
        on_device,
        mesh=mesh,
        in_specs=(rows,) * 6 + (P("grp"),),
        out_specs=(rows,) * 5,
        check_vma=False,
    )
```

time: 908 us -> 59.6 us (0.07); the launches traced: 893 us -> 59.4 us
  waiting for transfers between devices: 645 us -> 0 us
  matrix products: 77.2 us -> 0 us
  local copies, waits for them, and re-layouts: 70.4 us -> 0 us
  Pallas kernels: 0 us -> 58.7 us
  other arithmetic: 43.8 us -> 0 us
  starting transfers between devices: 41.7 us -> 0 us
  between operations: 15.2 us -> 0.64 us
    reduce_scatter x2 -> x0, waiting for transfers between devices: 437 us -> none  [the longest x1 287 us: on_device(): lax.psum_scatter(tail_part[1], 'seq', scatter_dimension=0, tiled=True)]
    all_gather x2 -> x0, waiting for transfers between devices: 138 us -> none  [the longest x1 91.6 us: on_device(): lax.all_gather(tail_values, 'seq', axis=0, tiled=True)]
    dot_general x50 -> x0, matrix products: 77.2 us -> none  [the longest x10 22.9 us: block_grads(): jnp.einsum('kgrc,rkgd->ckd', rounded, dout_heads, preferred_element_type=...]
    ppermute x16 -> x0, waiting for transfers between devices: 69.3 us -> none  [passed_along(): lax.ppermute(value, axis, [(source, source + steps) for source in range(l...]
    pallas_call x0 -> x2, Pallas kernels: none -> 58.7 us  [the longest x1 56.5 us: on_device(): pl.pallas_call(kernel, out_shape=(jax.ShapeDtypeStruct(queries.shape, BF1...]
    ppermute x16 -> x0, starting transfers between devices: 41.4 us -> none  [passed_along(): lax.ppermute(value, axis, [(source, source + steps) for source in range(l...]
    another operation x18 -> x0, local copies, waits for them, and re-layouts: 26.4 us -> none  [block_grads(): jnp.stack((key_grad, value_grad)).reshape(2, key_rows.shape[0], KVH * HD)]
    another operation x11 -> x0, other arithmetic: 19.1 us -> none  [the longest x8 14.2 us: block_grads(): jnp.stack((key_grad, value_grad)).reshape(2, key_rows.shape[0], KVH * HD)]
  transfers between devices with their start and end apart: 20 -> 0, of which waited for: 11 -> 0; matrix products, arithmetic and copies ran while one was open for 17% -> 0% of each run, Pallas kernels for 0% -> 0%
where the time goes in v2:
time: 59.6 us; the launch traced here: 59.4 us
  Pallas kernels  58.7 us (98%)
  between operations  0.64 us (1%)
    pallas_call x1, Pallas kernels, on_device(): pl.pallas_call(kernel, out_shape=(jax.ShapeDtypeStruct(queries.shape, BF1...  56.5 us
    pallas_call x1, Pallas kernels, on_device(): pl.pallas_call(write_out, out_shape=tuple((jax.ShapeDtypeStruct(x.shape,...  2.2 us

profile of v2, /device:TPU:1, one launch (start us, length us, event | category | flops | bytes accessed | tf_op | source)
XLA Modules:
  0.0 59.4 jit_solution(5256893820946920532)
XLA Ops:
  0.6 56.5 %shard_map.110 = (bf16[128,2048]{1,0:T(8,128)(2,1)}, bf16[128,1024]{1,0:T(8,128)(2,1)}, bf16[128,1024]{1,0:T(8,128)(2,1)}, bf16[16,1024]{1,0:T(8,128)(2,1)}, bf16[16,1024]{1,0:T(8,128)(2,1)}) custom-call(s32[2]{0:T(128)} %len_ref.1, bf16[128,2048]{1,0:T(8,128)(2,1)} %q_ref.1, bf16[128,2048]{1,0:T(8,128)(2,1)} %do_ref.1, bf16[128,1024]{1,0:T(8,128)(2,1)} %k_ref.1, ...), custom_call_target="tpu_custom_call" | custom-call | tf_op jit(solution)/shard_map/pallas_call | solution.py:649
  57.2 2.2 %shard_map.111 = (bf16[128,2048]{1,0:T(8,128)(2,1)}, bf16[128,1024]{1,0:T(8,128)(2,1)}, bf16[128,1024]{1,0:T(8,128)(2,1)}, bf16[16,1024]{1,0:T(8,128)(2,1)}, bf16[16,1024]{1,0:T(8,128)(2,1)}) custom-call(bf16[128,2048]{1,0:T(8,128)(2,1)} %get-tuple-element.10.refs_0_, bf16[128,1024]{1,0:T(8,128)(2,1)} %get-tuple-element.11.refs_1_, ...), custom_call_target="tpu_custom_call" | custom-call | tf_op jit(solution)/shard_map/pallas_call | solution.py:664

commit v3 on v2

--- a/solution.py
+++ b/solution.py
@@ -54,7 +54,7 @@
 
 def kernel(len_ref, q_ref, do_ref, k_ref, v_ref, tk_ref, tv_ref,
            dq_ref, dk_ref, dv_ref, dtk_ref, dtv_ref,
-           qb, dob, kv, tkv, kt, sc, dpc, ds, pr, dsx, prx, qq, oo, dqx,
+           qb, dob, kv, kvh, tkv, kt, sc, dpc, ds, pr, dsx, prx, qq, oo, dqx,
            tok, back, first_part, xsend, xrecv, hsend, hrecv, osend, dqs,
            txs, txr, tsend, trecv, tfin,
            in_send, in_recv, tg_send, tg_recv, ts_send, ts_recv, halo_send, halo_recv, sh_send, sh_recv,
@@ -65,8 +65,6 @@
     head = e // 2
     core = e % 2
     t0 = p * TOKENS
-    mine = pl.ds(core * HD, HD)
-    other = pl.ds((1 - core) * HD, HD)
     sibling = me + 1 - 2 * core
 
     def peer(t):
@@ -102,11 +100,10 @@
         return (q_ref, do_ref)[kind - 2].at[:, at128(to)]
 
     def target(kind, source, role):
-        columns = pl.ds(role * HD, HD)
         if kind == 0:
-            return tkv.at[at16(p * PLANE + source), columns]
+            return tkv.at[role, at16(p * PLANE + source), :]
         if kind == 1:
-            return kv.at[at128(W // ROWS + source), columns]
+            return kv.at[role, at128(W // ROWS + source), :]
         return (qb, dob)[kind - 2].at[at128(source), :]
 
     def give(kind, t, role):
@@ -152,41 +149,53 @@
 
     def tail_give(t):
         rows = at256(p)
-        return remote(tkv.at[rows, mine], tkv.at[rows, mine], tg_send.at[t], tg_recv.at[p], in_plane((p + t) % PLANES))
+        return remote(tkv.at[core, rows, :], tkv.at[core, rows, :], tg_send.at[t], tg_recv.at[p], in_plane((p + t) % PLANES))
 
     def tail_take(pp):
         rows = at256(pp)
-        return remote(tkv.at[rows, mine], tkv.at[rows, mine], tg_send.at[0], tg_recv.at[pp], in_plane(pp))
+        return remote(tkv.at[core, rows, :], tkv.at[core, rows, :], tg_send.at[0], tg_recv.at[pp], in_plane(pp))
 
     def tail_share(pp):
         rows = at256(pp)
-        return remote(tkv.at[rows, mine], tkv.at[rows, mine], ts_send.at[pp], ts_recv.at[pp], sibling)
+        return remote(tkv.at[core, rows, :], tkv.at[core, rows, :], ts_send.at[pp], ts_recv.at[pp], sibling)
 
     def tail_shared(pp):
         rows = at256(pp)
-        return remote(tkv.at[rows, mine], tkv.at[rows, other], ts_send.at[pp], ts_recv.at[pp], sibling)
+        return remote(tkv.at[core, rows, :], tkv.at[1 - core, rows, :], ts_send.at[pp], ts_recv.at[pp], sibling)
 
     def halo(k):
-        return remote(kv.at[pl.ds(TOKENS + k * GROUP, GROUP), mine], kv.at[pl.ds(k * GROUP, GROUP), mine],
+        return remote(kv.at[core, pl.ds(TOKENS + k * GROUP, GROUP), :], kvh.at[core, pl.ds(k * GROUP, GROUP), :],
                       halo_send.at[k], halo_recv.at[k], in_plane((p + 1) % PLANES))
+
+    def shared_ref(k):
+        return kvh if isinstance(k, int) and k < 2 else kv
 
     def share(k):
         rows = pl.ds(k * GROUP, GROUP)
-        return remote(kv.at[rows, mine], kv.at[rows, mine], sh_send.at[k], sh_recv.at[k], sibling)
+        ref = shared_ref(k)
+        return remote(ref.at[core, rows, :], ref.at[core, rows, :], sh_send.at[k], sh_recv.at[k], sibling)
 
     def shared(k):
         rows = pl.ds(k * GROUP, GROUP)
-        return remote(kv.at[rows, mine], kv.at[rows, other], sh_send.at[k], sh_recv.at[k], sibling)
+        ref = shared_ref(k)
+        return remote(ref.at[core, rows, :], ref.at[1 - core, rows, :], sh_send.at[k], sh_recv.at[k], sibling)
 
     give_all(0)
     give_all(1)
-    give_all(2)
-    give_all(3)
 
     take_some(0, 0, PLANE)
     for t in range(1, PLANES):
         tail_give(t).start()
     tail_share(p).start()
+
+    def sent(kind):
+        def body(t, carry):
+            give(kind, t, 0).wait_send()
+            return carry
+        lax.fori_loop(1, PLANE, body, 0)
+
+    sent(1)
+    give_all(2)
 
     for k in (5, 4, 3, 2):
         take_some(1, 4 * (k - 2), 4 * (k - 1))
@@ -223,33 +232,30 @@
     forth = (shift_col == shift_row + (ROWS - part)).astype(F32).astype(BF16)
     stream_row = lax.broadcasted_iota(jnp.int32, (ROWS, PAIR), 0)
 
-    def second_stream(n, carry):
+    def both(ref, n):
+        return jnp.concatenate([ref[0, at128(n), :], ref[1, at128(n), :]], axis=1)
+
+    def second_stream(n):
         low = jnp.clip(n - whole - 1, 0, W // ROWS - 1)
         high = jnp.clip(n - whole, 0, W // ROWS - 1)
-        moved = (dot_nn(forth[:, :ROWS], tkv[at128(low), :])
-                 + dot_nn(forth[:, ROWS:], tkv[at128(high), :]))
-        plain = kv[at128(n), :]
+        moved = (dot_nn(forth[:, :ROWS], both(tkv, low)) + dot_nn(forth[:, ROWS:], both(tkv, high)))
+        plain = both(kvh if n < W // ROWS else kv, n)
+        if n < W // ROWS:
+            kv[0, at128(n), :] = plain[:, :HD]
+            kv[1, at128(n), :] = plain[:, HD:]
         mixed = jnp.where(n * ROWS + stream_row < delta + W, moved, plain.astype(F32)).astype(BF16)
-        kv[at128(STREAM // ROWS + n), :] = mixed
+        kv[0, at128(STREAM // ROWS + n), :] = mixed[:, :HD]
+        kv[1, at128(STREAM // ROWS + n), :] = mixed[:, HD:]
         kt[:, at128(n)] = plain[:, :HD].T
         kt[:, at128(STREAM // ROWS + n)] = mixed[:, :HD].T
-        return carry
 
     for k in (5, 4, 3, 2):
         shared(k).wait_recv()
-        lax.fori_loop(4 * k, 4 * k + 4, second_stream, 0)
-
-    for k in (1, 0):
-        halo(k).wait_recv()
-        share(k).start()
-        shared(k).wait_recv()
-        share(k).wait_send()
-
-        @pl.when(p == 0)
-        def _(k=k):
-            kv[k * GROUP:(k + 1) * GROUP, :] = tkv[k * GROUP:(k + 1) * GROUP, :]
-
-        lax.fori_loop(4 * k, 4 * k + 4, second_stream, 0)
+        for n in range(4 * k, 4 * k + 4):
+            second_stream(n)
+        if k == 5:
+            sent(2)
+            give_all(3)
 
     key_row = lax.broadcasted_iota(jnp.int32, (ROWS, BLOCK), 0)
     query_row = lax.broadcasted_iota(jnp.int32, (ROWS, BLOCK), 1)
@@ -277,7 +283,7 @@
         qq[rows, HD:] = queries * second.astype(F32).astype(BF16)
         top = None
         for c in range(CHUNKS):
-            logits = dot_nt(kv[band(block, second, c), :HD], queries)
+            logits = dot_nt(kv[0, band(block, second, c), :], queries)
             if c < 2:
                 logits = jnp.where(key_row + c * ROWS > query_row, logits, NEG)
             if c >= CHUNKS - 2:
@@ -287,27 +293,57 @@
             top = most if top is None else jnp.maximum(top, most)
         return top
 
+    cut_row = lane_row + cut * BLOCK
+    in_cut = ((cut_row >= delta) & (cut * BLOCK < delta)).astype(F32)
+    inner = 7 * BLOCK
+
     def weigh(slot, top):
         total = jnp.zeros((1, BLOCK), F32)
         for c in range(CHUNKS):
             weight = jnp.exp2((sc[slot, c * ROWS:(c + 1) * ROWS, :] - top) * SCALE2)
             sc[slot, c * ROWS:(c + 1) * ROWS, :] = weight
             total = total + jnp.sum(weight, axis=0, keepdims=True)
-        return total
+        if slot == BLOCKS:
+            valid = in_cut
+        else:
+            valid = jnp.maximum((lane_row + slot * BLOCK < delta).astype(F32), is_second(slot).astype(F32))
+        inverse = valid / total
+        for c in range(CHUNKS):
+            rows = slice(c * ROWS, (c + 1) * ROWS)
+            probs = sc[slot, rows, :] * inverse
+            sc[slot, rows, :] = probs
+            if slot == BLOCKS:
+                prx[inner + c * ROWS:inner + (c + 1) * ROWS, :] = probs.astype(BF16)
+            else:
+                pr[slot, rows, :] = probs.astype(BF16)
+
+    def weigh_all(slots):
+        top = logits_of(slots[0])
+        for at, slot in enumerate(slots):
+            after = logits_of(slots[at + 1]) if at + 1 < len(slots) else None
+            weigh(slot, top)
+            top = after
+
+    weigh_all((7, 6, 5, 4))
+
+    for k in (1, 0):
+        halo(k).wait_recv()
+        share(k).start()
+    for k in (1, 0):
+        shared(k).wait_recv()
+        share(k).wait_send()
+
+        @pl.when(p == 0)
+        def _(k=k):
+            kvh[:, k * GROUP:(k + 1) * GROUP, :] = tkv[:, k * GROUP:(k + 1) * GROUP, :]
+
+        for n in range(4 * k, 4 * k + 4):
+            second_stream(n)
+
+    weigh_all((3, 2, 1, 0, BLOCKS))
 
     order = [BLOCKS] + list(range(BLOCKS))
-    totals = {}
-    tops = {order[0]: logits_of(order[0])}
-    for at, slot in enumerate(order):
-        if at + 1 < SLOTS:
-            tops[order[at + 1]] = logits_of(order[at + 1])
-        totals[slot] = weigh(slot, tops[slot])
-
     take_some(3, 0, PLANE)
-
-    cut_row = lane_row + cut * BLOCK
-    in_cut = ((cut_row >= delta) & (cut * BLOCK < delta)).astype(F32)
-    inner = 7 * BLOCK
 
     def turn(slot):
         return 0 if slot == BLOCKS else (slot + 1) % 2
@@ -321,28 +357,18 @@
         mixed = jnp.zeros((1, BLOCK), F32)
         for c in range(CHUNKS):
             rows = slice(c * ROWS, (c + 1) * ROWS)
-            dprob = dot_nt(kv[band(block, second, c), HD:], douts)
+            dprob = dot_nt(kv[1, band(block, second, c), :], douts)
             dpc[turn(slot), rows, :] = dprob
             mixed = mixed + jnp.sum(sc[slot, rows, :] * dprob, axis=0, keepdims=True)
         return mixed
 
-    def scores(slot, mixed):
-        if slot == BLOCKS:
-            valid = in_cut
-        else:
-            valid = jnp.maximum((lane_row + slot * BLOCK < delta).astype(F32), is_second(slot).astype(F32))
-        inverse = valid / totals[slot]
-        deltas = mixed / totals[slot]
+    def scores(slot, deltas):
         for c in range(CHUNKS):
             rows = slice(c * ROWS, (c + 1) * ROWS)
-            probs = sc[slot, rows, :] * inverse
-            dscores = (probs * (dpc[turn(slot), rows, :] - deltas)).astype(BF16)
+            dscores = (sc[slot, rows, :] * (dpc[turn(slot), rows, :] - deltas)).astype(BF16)
             if slot == BLOCKS:
-                rows = slice(inner + c * ROWS, inner + (c + 1) * ROWS)
-                prx[rows, :] = probs.astype(BF16)
-                dsx[rows, :] = dscores
+                dsx[inner + c * ROWS:inner + (c + 1) * ROWS, :] = dscores
             else:
-                pr[slot, rows, :] = probs.astype(BF16)
                 ds[slot, rows, :] = dscores
 
     def query_grad(slot):
@@ -358,7 +384,7 @@
         return remote(dqs.at[at128(n), :], dq_ref.at[:, at128(e)], out_send.at[0, n], out_recv.at[0, e], p * PLANE + n)
 
     def swap(u):
-        return remote(xsend.at[at256(u), other], xrecv.at[at256(u), :], x_send.at[u], x_recv.at[u], sibling)
+        return remote(xsend.at[1 - core, at256(u), :], xrecv.at[at256(u), :], x_send.at[u], x_recv.at[u], sibling)
 
     def send_halo_grad(u):
         return remote(hsend.at[at256(u), :], hrecv.at[at256(u), :], hg_send.at[u], hg_recv.at[u],
@@ -393,20 +419,20 @@
         token = []
         for ref, ref_x, right_side, scale in ((ds, dsx, qq, SCALE), (pr, prx, oo, 1.0)):
             parts = [ref[i, (u - i) * BLOCK:(u - i + 1) * BLOCK, :] for i in range(low, high + 1)]
-            both = dot_nn(jnp.concatenate(parts, axis=1), right_side[low * BLOCK:(high + 1) * BLOCK, :])
-            both = (both + dot_nn(ref_x[extra, :], right_side[BLOCKS * BLOCK:, :])) * scale
-            token.append(both[:, :HD] + jnp.where(later, both[:, HD:], 0.0))
+            sides = dot_nn(jnp.concatenate(parts, axis=1), right_side[low * BLOCK:(high + 1) * BLOCK, :])
+            sides = (sides + dot_nn(ref_x[extra, :], right_side[BLOCKS * BLOCK:, :])) * scale
+            token.append(sides[:, :HD] + jnp.where(later, sides[:, HD:], 0.0))
         rows = slice(u * BLOCK, (u + 1) * BLOCK)
-        token = jnp.concatenate(token, axis=1)
-        tok[u % 4] = token
-        xsend[rows, :] = token.astype(BF16)
+        for kind in range(2):
+            tok[u % 4, kind] = token[kind]
+            xsend[kind, rows, :] = token[kind].astype(BF16)
+            if u < HALO_UNITS:
+                first_part[rows, kind * HD:(kind + 1) * HD] = (token[kind] * is_first).astype(BF16)
         swap(u).start()
-        if u < HALO_UNITS:
-            first_part[rows, :] = (token * is_first).astype(BF16)
 
     def settle(u):
         swap(u).wait_recv()
-        total = tok[u % 4, :, mine] + xrecv[u * BLOCK:(u + 1) * BLOCK, :].astype(F32)
+        total = tok[u % 4, core] + xrecv[u * BLOCK:(u + 1) * BLOCK, :].astype(F32)
         if u < HALO_UNITS:
             hsend[u * BLOCK:(u + 1) * BLOCK, :] = (total * has_halo).astype(BF16)
             send_halo_grad(u).start()
@@ -444,7 +470,7 @@
         back[k * BLOCK:(k + 1) * BLOCK, :] = jnp.concatenate(token, axis=1).astype(BF16)
 
     def swap_tail(pp):
-        return remote(txs.at[at256(pp), other], txr.at[at256(pp), :], tx_send.at[pp], tx_recv.at[pp], sibling)
+        return remote(txs.at[1 - core, at256(pp), :], txr.at[at256(pp), :], tx_send.at[pp], tx_recv.at[pp], sibling)
 
     def send_tail(pp):
         return remote(tsend.at[at256(pp), :], trecv.at[at256(p), :], tr_send.at[pp], tr_recv.at[p], in_plane(pp))
@@ -459,7 +485,9 @@
         for pp in range(PLANES):
             rows = slice(pp * BLOCK, (pp + 1) * BLOCK)
             moved = dot_nn(hit, back[pp * BLOCK:(pp + 2) * BLOCK, :])
-            txs[rows, :] = (moved + first_part[rows, :].astype(F32)).astype(BF16)
+            moved = (moved + first_part[rows, :].astype(F32)).astype(BF16)
+            txs[0, rows, :] = moved[:, :HD]
+            txs[1, rows, :] = moved[:, HD:]
         for pp in range(PLANES):
             swap_tail(pp).start()
 
@@ -468,7 +496,7 @@
             swap_tail(pp).wait_recv()
         for pp in range(PLANES):
             rows = slice(pp * BLOCK, (pp + 1) * BLOCK)
-            tsend[rows, :] = (txs[rows, mine].astype(F32) + txr[rows, :].astype(F32)).astype(BF16)
+            tsend[rows, :] = (txs[core, rows, :].astype(F32) + txr[rows, :].astype(F32)).astype(BF16)
         for pp in range(PLANES):
             @pl.when(p != pp)
             def _(pp=pp):
@@ -489,13 +517,17 @@
         if slot == 5:
             for u in range(4):
                 settle(u)
+            gather(4)
+            gather(5)
     query_grad(BLOCKS - 1)
     start_tail_sums()
     lax.fori_loop(12, PLANE, send_some_dq, 0)
-    gather(4)
-    gather(5)
+    gather(6)
+    gather(7)
+    settle(4)
+    settle(5)
     send_tail_sums()
-    for u in range(6, UNITS):
+    for u in range(8, UNITS):
         gather(u)
         settle(u - 2)
     settle(UNITS - 2)
@@ -538,7 +570,7 @@
 
     def finish_sends(t, carry):
         n = (e + t) % PLANE
-        for kind in range(4):
+        for kind in (0, 3):
             give(kind, t, 0).wait_send()
         send_dq(n).wait_send()
         send_own(n, 0).wait_send()
@@ -613,8 +645,9 @@
     scratch = [
         pltpu.VMEM((TOKENS, HD), BF16),
         pltpu.VMEM((TOKENS, HD), BF16),
-        pltpu.VMEM((2 * STREAM, PAIR), BF16),
-        pltpu.VMEM((W, PAIR), BF16),
+        pltpu.VMEM((2, 2 * STREAM, HD), BF16),
+        pltpu.VMEM((2, W, HD), BF16),
+        pltpu.VMEM((2, W, HD), BF16),
         pltpu.VMEM((HD, 2 * STREAM), BF16),
         pltpu.VMEM((SLOTS, BAND, BLOCK), F32),
         pltpu.VMEM((2, BAND, BLOCK), F32),
@@ -625,16 +658,16 @@
         pltpu.VMEM((SLOTS * BLOCK, PAIR), BF16),
         pltpu.VMEM((SLOTS * BLOCK, PAIR), BF16),
         pltpu.VMEM((BLOCK, HD), F32),
-        pltpu.VMEM((4, BLOCK, PAIR), F32),
+        pltpu.VMEM((4, 2, BLOCK, HD), F32),
         pltpu.VMEM((W + BLOCK, PAIR), BF16),
         pltpu.VMEM((W, PAIR), BF16),
-        pltpu.VMEM((STREAM, PAIR), BF16),
+        pltpu.VMEM((2, STREAM, HD), BF16),
         pltpu.VMEM((STREAM, HD), BF16),
         pltpu.VMEM((W, HD), BF16),
         pltpu.VMEM((W, HD), BF16),
         pltpu.VMEM((TOKENS, HD), BF16),
         pltpu.VMEM((TOKENS, HD), BF16),
-        pltpu.VMEM((W, PAIR), BF16),
+        pltpu.VMEM((2, W, HD), BF16),
         pltpu.VMEM((W, HD), BF16),
         pltpu.VMEM((W, HD), BF16),
         pltpu.VMEM((W, HD), BF16),

time: 59.6 us -> 57.8 us (0.970)
  Pallas kernels: 58.7 us -> 57 us
    pallas_call x1, Pallas kernels: 56.5 us -> 54.8 us  [on_device(): pl.pallas_call(kernel, out_shape=(jax.ShapeDtypeStruct(queries.shape, BF1...]
where the time goes in v3:
time: 57.8 us; the launch traced here: 57.6 us
  Pallas kernels  57 us (99%)
  between operations  0.64 us (1%)
    pallas_call x1, Pallas kernels, on_device(): pl.pallas_call(kernel, out_shape=(jax.ShapeDtypeStruct(queries.shape, BF1...  54.8 us
    pallas_call x1, Pallas kernels, on_device(): pl.pallas_call(write_out, out_shape=tuple((jax.ShapeDtypeStruct(x.shape,...  2.2 us

profile of v3, /device:TPU:1, one launch (start us, length us, event | category | flops | bytes accessed | tf_op | source)
XLA Modules:
  0.0 57.6 jit_solution(15881139213601208224)
XLA Ops:
  0.6 54.8 %shard_map.110 = (bf16[128,2048]{1,0:T(8,128)(2,1)}, bf16[128,1024]{1,0:T(8,128)(2,1)}, bf16[128,1024]{1,0:T(8,128)(2,1)}, bf16[16,1024]{1,0:T(8,128)(2,1)}, bf16[16,1024]{1,0:T(8,128)(2,1)}) custom-call(s32[2]{0:T(128)} %len_ref.1, bf16[128,2048]{1,0:T(8,128)(2,1)} %q_ref.1, bf16[128,2048]{1,0:T(8,128)(2,1)} %do_ref.1, bf16[128,1024]{1,0:T(8,128)(2,1)} %k_ref.1, ...), custom_call_target="tpu_custom_call" | custom-call | tf_op jit(solution)/shard_map/pallas_call | solution.py:682
  55.4 2.2 %shard_map.111 = (bf16[128,2048]{1,0:T(8,128)(2,1)}, bf16[128,1024]{1,0:T(8,128)(2,1)}, bf16[128,1024]{1,0:T(8,128)(2,1)}, bf16[16,1024]{1,0:T(8,128)(2,1)}, bf16[16,1024]{1,0:T(8,128)(2,1)}) custom-call(bf16[128,2048]{1,0:T(8,128)(2,1)} %get-tuple-element.10.refs_0_, bf16[128,1024]{1,0:T(8,128)(2,1)} %get-tuple-element.11.refs_1_, ...), custom_call_target="tpu_custom_call" | custom-call | tf_op jit(solution)/shard_map/pallas_call | solution.py:697

commit v4 on v3

--- a/solution.py
+++ b/solution.py
@@ -539,6 +539,45 @@
         def _(role=role):
             keep_own(role).start()
 
+    def finish_early(t, carry):
+        n = (e + t) % PLANE
+        for kind in (0, 3):
+            give(kind, t, 0).wait_send()
+        send_dq(n).wait_send()
+        remote(dqs.at[at128(e), :], dq_ref.at[:, at128(n)], out_send.at[0, n], out_recv.at[0, n], peer(t)).wait_recv()
+        return carry
+
+    lax.fori_loop(1, PLANE, finish_early, 0)
+
+    def finish_units(u, carry):
+        swap(u).wait_send()
+        return carry
+
+    lax.fori_loop(0, UNITS, finish_units, 0)
+
+    def finish_halo(k, carry):
+        halo(k).wait_send()
+        return carry
+
+    lax.fori_loop(0, 2, finish_halo, 0)
+
+    def finish_share(k, carry):
+        share(k).wait_send()
+        return carry
+
+    lax.fori_loop(2, 6, finish_share, 0)
+
+    def finish_planes(pp, carry):
+        send_halo_grad(pp).wait_send()
+        tail_share(pp).wait_send()
+        swap_tail(pp).wait_send()
+        return carry
+
+    lax.fori_loop(0, PLANES, finish_planes, 0)
+    for t in range(1, PLANES):
+        tail_give(t).wait_send()
+    keep_dq().wait()
+
     summed = tsend[at256(p), :].astype(F32)
     for t in range(1, PLANES):
         pp = (p + t) % PLANES
@@ -569,50 +608,20 @@
             keep_tail_out(role).start()
 
     def finish_sends(t, carry):
-        n = (e + t) % PLANE
-        for kind in (0, 3):
-            give(kind, t, 0).wait_send()
-        send_dq(n).wait_send()
-        send_own(n, 0).wait_send()
+        send_own((e + t) % PLANE, 0).wait_send()
         send_tail_out(t, 0).wait_send()
-        remote(dqs.at[at128(e), :], dq_ref.at[:, at128(n)], out_send.at[0, n], out_recv.at[0, n], peer(t)).wait_recv()
         return carry
 
     lax.fori_loop(1, PLANE, finish_sends, 0)
 
-    def finish_units(u, carry):
-        swap(u).wait_send()
-        return carry
-
-    lax.fori_loop(0, UNITS, finish_units, 0)
-
-    def finish_halo(k, carry):
-        halo(k).wait_send()
-        return carry
-
-    lax.fori_loop(0, 2, finish_halo, 0)
-
-    def finish_share(k, carry):
-        share(k).wait_send()
-        return carry
-
-    lax.fori_loop(2, 6, finish_share, 0)
-
-    def finish_planes(pp, carry):
-        send_halo_grad(pp).wait_send()
-        tail_share(pp).wait_send()
-        swap_tail(pp).wait_send()
-
+    def finish_tail(pp, carry):
         @pl.when(p != pp)
         def _():
             send_tail(pp).wait_send()
 
         return carry
 
-    lax.fori_loop(0, PLANES, finish_planes, 0)
-    for t in range(1, PLANES):
-        tail_give(t).wait_send()
-    keep_dq().wait()
+    lax.fori_loop(0, PLANES, finish_tail, 0)
 
     def finish_heads(n, carry):
         columns = at128(n)

time: 57.8 us -> 57.8 us (level)
  no operation moved by 1% of the time
where the time goes in v4:
time: 57.8 us; the launch traced here: 57.6 us
  Pallas kernels  57 us (99%)
  between operations  0.64 us (1%)
    pallas_call x1, Pallas kernels, on_device(): pl.pallas_call(kernel, out_shape=(jax.ShapeDtypeStruct(queries.shape, BF1...  54.8 us
    pallas_call x1, Pallas kernels, on_device(): pl.pallas_call(write_out, out_shape=tuple((jax.ShapeDtypeStruct(x.shape,...  2.2 us

profile of v4, /device:TPU:1, one launch (start us, length us, event | category | flops | bytes accessed | tf_op | source)
XLA Modules:
  0.0 57.6 jit_solution(9850828204233640394)
XLA Ops:
  0.6 54.8 %shard_map.110 = (bf16[128,2048]{1,0:T(8,128)(2,1)}, bf16[128,1024]{1,0:T(8,128)(2,1)}, bf16[128,1024]{1,0:T(8,128)(2,1)}, bf16[16,1024]{1,0:T(8,128)(2,1)}, bf16[16,1024]{1,0:T(8,128)(2,1)}) custom-call(s32[2]{0:T(128)} %len_ref.1, bf16[128,2048]{1,0:T(8,128)(2,1)} %q_ref.1, bf16[128,2048]{1,0:T(8,128)(2,1)} %do_ref.1, bf16[128,1024]{1,0:T(8,128)(2,1)} %k_ref.1, ...), custom_call_target="tpu_custom_call" | custom-call | tf_op jit(solution)/shard_map/pallas_call | solution.py:691
  55.4 2.2 %shard_map.111 = (bf16[128,2048]{1,0:T(8,128)(2,1)}, bf16[128,1024]{1,0:T(8,128)(2,1)}, bf16[128,1024]{1,0:T(8,128)(2,1)}, bf16[16,1024]{1,0:T(8,128)(2,1)}, bf16[16,1024]{1,0:T(8,128)(2,1)}) custom-call(bf16[128,2048]{1,0:T(8,128)(2,1)} %get-tuple-element.10.refs_0_, bf16[128,1024]{1,0:T(8,128)(2,1)} %get-tuple-element.11.refs_1_, ...), custom_call_target="tpu_custom_call" | custom-call | tf_op jit(solution)/shard_map/pallas_call | solution.py:706
